TPU v7x, 128 devices: a whole 4x4x4 slice. The times are simulated.
128 devices in a mesh: dp: 32 (over z, x, core), seq: 4 (over y).
Axes of the slice: x: 4, y: 4, z: 4, core: 2. Of those that a mesh axis runs over, the one named last changes fastest.
Arguments:
- tokens: bfloat16 [32, 1024, 1024], P('dp', 'seq'), may hold values from -6 to 6
- captions: bfloat16 [32, 128, 1024], P('dp', None, 'seq'), may hold values from -6 to 6
- cap_lengths: int32 [32], P('dp'), may hold values from 1 to 128, as said below
- w_qkv: bfloat16 [1024, 3072], P(('dp', 'seq')), may hold values from -0.1875 to 0.1875
- w_self_out: bfloat16 [1024, 1024], P(('dp', 'seq')), may hold values from -1 to 1
- w_cross_q: bfloat16 [1024, 1024], P(('dp', 'seq')), may hold values from -0.1875 to 0.1875
- w_cross_kv: bfloat16 [1024, 2048], P(('dp', 'seq')), may hold values from -0.1875 to 0.1875
- w_cross_out: bfloat16 [1024, 1024], P(('dp', 'seq')), may hold values from -0.5 to 0.5
- w_in: bfloat16 [1024, 4096], P(('dp', 'seq')), may hold values from -0.1875 to 0.1875
- w_out: bfloat16 [4096, 1024], P(('dp', 'seq')), may hold values from -0.09375 to 0.09375
- norm_gains: bfloat16 [3, 1024], P(None, ('dp', 'seq')), may hold values from 0.5 to 1.5
- norm_shifts: bfloat16 [3, 1024], P(None, ('dp', 'seq')), may hold values from -4 to 4
- out_biases: bfloat16 [3, 1024], P(None, ('dp', 'seq')), may hold values from -4 to 4
- in_bias: bfloat16 [4096], P(('dp', 'seq')), may hold values from -6 to 6
- out_grad: bfloat16 [32, 1024, 1024], P('dp', 'seq'), may hold values from -6 to 6
Outputs:
- layer_out: bfloat16 [32, 1024, 1024], P('dp', 'seq')
- tokens_grad: float32 [32, 1024, 1024], P('dp', 'seq')
- captions_grad: float32 [32, 128, 1024], P('dp', None, 'seq')
- w_qkv_grad: float32 [1024, 3072], P(('dp', 'seq'))
- w_self_out_grad: float32 [1024, 1024], P(('dp', 'seq'))
- w_cross_q_grad: float32 [1024, 1024], P(('dp', 'seq'))
- w_cross_kv_grad: float32 [1024, 2048], P(('dp', 'seq'))
- w_cross_out_grad: float32 [1024, 1024], P(('dp', 'seq'))
- w_in_grad: float32 [1024, 4096], P(('dp', 'seq'))
- w_out_grad: float32 [4096, 1024], P(('dp', 'seq'))
- norm_gains_grad: float32 [3, 1024], P(None, ('dp', 'seq'))
- norm_shifts_grad: float32 [3, 1024], P(None, ('dp', 'seq'))
- out_biases_grad: float32 [3, 1024], P(None, ('dp', 'seq'))
- in_bias_grad: float32 [4096], P(('dp', 'seq'))
Inputs may be any that keep to these rules, and one draw needn't show every extreme that they name: `cap_lengths`: in every draw some image attends to all 128 caption rows.
All inputs are finite; a program needn't handle non-finite values.
Results may differ from a plain program's by a relative error of at most 0.019.
Values may be sent and summed in bfloat16 or wider, within the bound.
A program may use at most 384 MiB of HBM per device.

v0:
```python
import functools

import jax
import jax.numpy as jnp
from jax import lax
from jax.experimental import pallas as pl
from jax.experimental.pallas import tpu as pltpu
from jax.sharding import PartitionSpec as P

MESH = pl.DeviceIdType.MESH
def position():
    dp, y = lax.axis_index("dp"), lax.axis_index("seq")
    return {"z": lax.div(dp, 8), "x": lax.rem(lax.div(dp, 2), 4), "c": lax.rem(dp, 2), "y": y}


def device(at):
    return (at["z"] * 8 + at["x"] * 2 + at["c"], at["y"])


def moved(at, axis, by):
    size = 2 if axis == "c" else 4
    return {**at, axis: lax.rem(at[axis] + by + size, size)}


class Copies:
    def __init__(self, send, recv):
        self.send, self.recv, self.used = send, recv, 0

    def start(self, src, dst, at):
        k = self.used
        self.used += 1
        copy = pltpu.make_async_remote_copy(src_ref=src, dst_ref=dst, send_sem=self.send.at[k], recv_sem=self.recv.at[k], device_id=device(at), device_id_type=MESH)
        copy.start()
        return copy


def block(ref, at, whole, cols, **fixed):
    idx = []
    for axis in ("z", "x", "c", "y"):
        idx.append(fixed[axis] if axis in fixed else slice(None) if axis in whole else at[axis])
    return ref.at[(*idx, slice(None), cols)]


def gather_flow(ref, at, cols, axes, whole, copies, partner, done):
    whole = set(whole)
    for axis in axes:
        up, down = moved(at, axis, 1), moved(at, axis, -1)
        own = block(ref, at, whole, cols)
        a = copies.start(own, own, up)
        b = copies.start(own, own, down)
        yield
        a.wait_recv()
        b.wait_recv()
        low = block(ref, down, whole, cols, c=0)
        high = block(ref, up, whole, cols, c=1)
        c = copies.start(low, low, up)
        d = copies.start(high, high, down)
        for p in (down, up):
            got = block(ref, p, whole, cols)
            done.append(copies.start(got, got, partner))
        yield
        c.wait_recv()
        d.wait_recv()
        far = block(ref, moved(at, axis, 2), whole, cols)
        done.append(copies.start(far, far, partner))
        for s in (a, b, c, d):
            s.wait_send()
        whole.add(axis)


EPSILON = 1e-05
MASKED = -1e30
SCALE = 64 ** -0.5
BF, F32 = jnp.bfloat16, jnp.float32
def mm(a, b):
    return jnp.dot(a, b, preferred_element_type=F32)


def mm_rows(a, b):
    return lax.dot_general(a, b, (((0,), (0,)), ((), ())), preferred_element_type=F32)


def mm_cols(a, b):
    return lax.dot_general(a, b, (((1,), (1,)), ((), ())), preferred_element_type=F32)


def normed(v):
    centred = v - jnp.mean(v, axis=-1, keepdims=True)
    r = lax.rsqrt(jnp.mean(centred * centred, axis=-1, keepdims=True) + EPSILON)
    return centred * r, r


def norm_back(v, d, gain):
    z, r = normed(v)
    w = d * gain
    dv = r * (w - jnp.mean(w, axis=-1, keepdims=True) - z * jnp.mean(w * z, axis=-1, keepdims=True))
    return dv, jnp.sum(d * z, axis=0, keepdims=True), jnp.sum(d, axis=0, keepdims=True)


def loop(n, body):
    def step(i, _):
        body(i)
        return 0

    lax.fori_loop(0, n, step, 0)


def gelu_both(h):
    cdf = 0.5 * (1.0 + lax.erf(h * (0.5 ** 0.5)))
    return h * cdf, cdf + h * jnp.exp(-0.5 * h * h) * (1.0 / (2.0 * 3.141592653589793) ** 0.5)


def lanes_of(pair_shape, head):
    lane = lax.broadcasted_iota(jnp.int32, pair_shape, 1)
    return (lane < 64) if head == 0 else (lane >= 64)


def middle_kernel(length, x_in, att_in, dy_in, ck_in, cv_in, vec, inb, wc, win, wout,
                  out, dx1_o, datt_o, dckv_o, n2_o, n3_o, catt_o, u_o, dh_o, r1_o, r2_o, dcq_o, sums, dinb,
                  so, wcq, co, wi, wo, x1, x2, probs, cq, ya, dn, dca, sem):
    loads = []
    for k, dst in enumerate((so, wcq, co)):
        loads.append(pltpu.make_async_copy(wc.at[:, pl.ds(k * 1024, 1024)], dst, sem.at[k]))
    for l in loads:
        l.start()
    chunk = 512
    n_chunk = wi.shape[1] // chunk

    def ff_loads(i):
        cols = pl.ds(pl.multiple_of(i * chunk, chunk), chunk)
        return (pltpu.make_async_copy(win.at[:, cols], wi.at[:, cols], sem.at[3 + 2 * i]),
                pltpu.make_async_copy(wout.at[cols], wo.at[cols], sem.at[4 + 2 * i]))

    for i in range(n_chunk):
        for l in ff_loads(i):
            l.start()

    step_rows = 64
    def by_rows(body):
        loop(256 // step_rows, lambda i: body(pl.ds(pl.multiple_of(i * step_rows, step_rows), step_rows)))

    def row(k):
        return vec[k:k + 1, :]

    sums[...] = jnp.zeros_like(sums)

    loads[0].wait()
    x1[...] = mm(att_in[...], so[...])

    def after_self(r):
        v = x_in[r, :].astype(F32) + x1[r, :] + row(6)
        x1[r, :] = v
        z, _ = normed(v)
        n2_o[r, :] = (z * row(1) + row(4)).astype(BF)

    by_rows(after_self)
    loads[1].wait()
    cq[...] = mm(n2_o[...], wcq[...]).astype(BF)

    seen = lax.broadcasted_iota(jnp.int32, (128, 256), 0) < length[0]

    def cross_forward(p):
        cols = pl.ds(pl.multiple_of(p * 128, 128), 128)
        k, v, q = ck_in[:, cols], cv_in[:, cols], cq[:, cols]
        mixed = []
        for head in range(2):
            qh = jnp.where(lanes_of(q.shape, head), q, jnp.zeros_like(q))
            s = jnp.where(seen, mm_cols(k, qh) * SCALE, MASKED)
            e = jnp.exp(s - jnp.max(s, axis=0, keepdims=True))
            prob = e / jnp.sum(e, axis=0, keepdims=True)
            probs[2 * p + head] = prob
            mixed.append(mm_rows(prob.astype(BF), v))
        catt_o[:, cols] = jnp.where(lanes_of(q.shape, 0), mixed[0], mixed[1]).astype(BF)

    loop(8, cross_forward)
    loads[2].wait()
    x2[...] = mm(catt_o[...], co[...])

    def after_cross(r):
        v = x1[r, :] + x2[r, :] + row(7)
        x2[r, :] = v
        z, _ = normed(v)
        n3_o[r, :] = (z * row(2) + row(5)).astype(BF)

    by_rows(after_cross)

    ya[...] = jnp.zeros_like(ya)
    dn[...] = jnp.zeros_like(dn)

    def feed(i):
        for l in ff_loads(i):
            l.wait()
        cols = pl.ds(pl.multiple_of(i * chunk, chunk), chunk)
        h = mm(n3_o[...], wi[:, cols]) + inb[:, cols]
        u, slope = gelu_both(h)
        u = u.astype(BF)
        u_o[:, cols] = u
        ya[...] += mm(u, wo[cols, :])
        dh = (mm_cols(dy_in[...], wo[cols, :]) * slope).astype(BF)
        dh_o[:, cols] = dh
        dinb[:, cols] = jnp.sum(dh.astype(F32), axis=0, keepdims=True)
        dn[...] += mm_cols(dh, wi[:, cols])

    loop(n_chunk, feed)

    def after_feed(r):
        v = x2[r, :]
        out[r, :] = (v + ya[r, :] + row(8)).astype(BF)
        dy = dy_in[r, :].astype(F32)
        dv, dgain, dshift = norm_back(v, dn[r, :], row(2))
        d = dy + dv
        x2[r, :] = d
        r2_o[r, :] = d.astype(BF)
        sums[2:3, :] += dgain
        sums[5:6, :] += dshift
        sums[7:8, :] += jnp.sum(d, axis=0, keepdims=True)
        sums[8:9, :] += jnp.sum(dy, axis=0, keepdims=True)

    by_rows(after_feed)

    dca[...] = mm_cols(r2_o[...], co[...]).astype(BF)

    def cross_backward(p):
        cols = pl.ds(pl.multiple_of(p * 128, 128), 128)
        k, v, q, d = ck_in[:, cols], cv_in[:, cols], cq[:, cols], dca[:, cols]
        dk = dv = jnp.zeros((128, 128), F32)
        dq = []
        for head in range(2):
            lanes = lanes_of(q.shape, head)
            qh = jnp.where(lanes, q, jnp.zeros_like(q))
            dout = jnp.where(lanes, d, jnp.zeros_like(d))
            prob = probs[2 * p + head]
            dp = mm_cols(v, dout)
            ds = (prob * (dp - jnp.sum(dp * prob, axis=0, keepdims=True))).astype(BF)
            dv += mm(prob.astype(BF), dout)
            dk += mm(ds, qh)
            dq.append(mm_rows(ds, k))
        dcq_o[:, cols] = (jnp.where(lanes_of(q.shape, 0), dq[0], dq[1]) * SCALE).astype(BF)
        dckv_o[:, cols] = (dk * SCALE).astype(BF)
        dckv_o[:, pl.ds(pl.multiple_of(1024 + p * 128, 128), 128)] = dv.astype(BF)

    loop(8, cross_backward)
    dn[...] = mm_cols(dcq_o[...], wcq[...])

    def before_cross(r):
        dv, dgain, dshift = norm_back(x1[r, :], dn[r, :], row(1))
        d = x2[r, :] + dv
        dx1_o[r, :] = d
        r1_o[r, :] = d.astype(BF)
        sums[1:2, :] += dgain
        sums[4:5, :] += dshift
        sums[6:7, :] += jnp.sum(d, axis=0, keepdims=True)

    by_rows(before_cross)
    datt_o[...] = mm_cols(r1_o[...], so[...]).astype(BF)


def middle(length, x, att, dy, ck, cv, vec, inb, wc, win, wout):
    s = jax.ShapeDtypeStruct
    outs = [s((256, 1024), BF), s((256, 1024), F32), s((256, 1024), BF), s((128, 2048), BF), s((256, 1024), BF), s((256, 1024), BF),
            s((256, 1024), BF), s((256, 4096), BF), s((256, 4096), BF), s((256, 1024), BF), s((256, 1024), BF), s((256, 1024), BF),
            s((16, 1024), F32), s((1, 4096), F32)]
    vm, anywhere = pl.BlockSpec(memory_space=pltpu.VMEM), pl.BlockSpec(memory_space=pl.ANY)
    scratch = [pltpu.VMEM((1024, 1024), BF)] * 3 + [pltpu.VMEM((1024, 4096), BF), pltpu.VMEM((4096, 1024), BF)]
    scratch += [pltpu.VMEM((256, 1024), F32)] * 2 + [pltpu.VMEM((16, 128, 256), F32), pltpu.VMEM((256, 1024), BF)]
    scratch += [pltpu.VMEM((256, 1024), F32)] * 2 + [pltpu.VMEM((256, 1024), BF), pltpu.SemaphoreType.DMA((19,))]
    return pl.pallas_call(
        middle_kernel, out_shape=outs,
        in_specs=[pl.BlockSpec(memory_space=pltpu.SMEM)] + [vm] * 7 + [anywhere] * 3, out_specs=[vm] * len(outs),
        scratch_shapes=scratch, compiler_params=pltpu.CompilerParams(vmem_limit_bytes=60 << 20),
        name="middle",
    )(length, x, att, dy, ck, cv, vec, inb, wc, win, wout)


BLOCK = 256
def causal_keep(n, at):
    keys = lax.broadcasted_iota(jnp.int32, (n, BLOCK), 0)
    return keys <= lax.broadcasted_iota(jnp.int32, (n, BLOCK), 1) + at


def project(x, wq, vec, n1, qkv):
    def rows(i):
        r = pl.ds(pl.multiple_of(i * 128, 128), 128)
        z, _ = normed(x[r, :].astype(F32))
        n1[r, :] = (z * vec[0:1, :] + vec[3:4, :]).astype(BF)

    loop(8, rows)

    def cols(i):
        r = pl.ds(pl.multiple_of(i * BLOCK, BLOCK), BLOCK)
        qkv[r, :] = mm(n1[r, :], wq[:, 0:768]).astype(BF)

    loop(4, cols)


def self_forward(qkv, att, lse):
    def pair(p):
        for i in range(1024 // BLOCK):
            n, r = (i + 1) * BLOCK, slice(i * BLOCK, (i + 1) * BLOCK)
            at = lambda part: pl.ds(pl.multiple_of(part * 256 + p * 128, 128), 128)
            q, k, v = qkv[r, at(0)], qkv[0:n, at(1)], qkv[0:n, at(2)]
            keep = causal_keep(n, i * BLOCK)
            mixed = []
            for head in range(2):
                qh = jnp.where(lanes_of(q.shape, head), q, jnp.zeros_like(q))
                s = jnp.where(keep, mm_cols(k, qh) * SCALE, MASKED)
                top = jnp.max(s, axis=0, keepdims=True)
                e = jnp.exp(s - top)
                total = jnp.sum(e, axis=0, keepdims=True)
                lse[2 * p + head, :, r] = top + jnp.log(total)
                mixed.append(mm_rows((e * (1.0 / total)).astype(BF), v))
            att[r, at(0)] = jnp.where(lanes_of(q.shape, 0), mixed[0], mixed[1]).astype(BF)

    loop(2, pair)


def self_backward(qkv, lse, datt, dqkv, dk, dv):
    def pair(p):
        at = lambda part: pl.ds(pl.multiple_of(part * 256 + p * 128, 128), 128)
        dk[...] = jnp.zeros_like(dk)
        dv[...] = jnp.zeros_like(dv)
        for i in range(1024 // BLOCK):
            n, r = (i + 1) * BLOCK, slice(i * BLOCK, (i + 1) * BLOCK)
            q, k, v, d = qkv[r, at(0)], qkv[0:n, at(1)], qkv[0:n, at(2)], datt[r, at(0)]
            keep = causal_keep(n, i * BLOCK)
            dq = []
            for head in range(2):
                lanes = lanes_of(q.shape, head)
                qh = jnp.where(lanes, q, jnp.zeros_like(q))
                dout = jnp.where(lanes, d, jnp.zeros_like(d))
                prob = jnp.where(keep, jnp.exp(mm_cols(k, qh) * SCALE - lse[2 * p + head, :, r]), 0.0)
                dp = mm_cols(v, dout)
                ds = (prob * (dp - jnp.sum(dp * prob, axis=0, keepdims=True))).astype(BF)
                dv[0:n, :] += mm(prob.astype(BF), dout)
                dk[0:n, :] += mm(ds, qh)
                dq.append(mm_rows(ds, k))
            dqkv[r, at(0)] = (jnp.where(lanes_of(q.shape, 0), dq[0], dq[1]) * SCALE).astype(BF)
        dqkv[:, at(1)] = (dk[...] * SCALE).astype(BF)
        dqkv[:, at(2)] = dv[...].astype(BF)

    loop(2, pair)


def greet(others):
    barrier = pltpu.get_barrier_semaphore()
    for o in others:
        pl.semaphore_signal(barrier, inc=1, device_id=device(o), device_id_type=MESH)
    pl.semaphore_wait(barrier, len(others))


def half(n, of):
    return pl.ds(pl.multiple_of(of["c"] * (n // 2), 128), n // 2)


def finish(flows):
    live = list(flows)
    while live:
        for f in list(live):
            if next(f, "end") == "end":
                live.remove(f)


def quarter(of):
    return pl.ds(pl.multiple_of(of["y"] * 256, 256), 256)


def gather_kernel(c_in, win_in, wout_in, q_in, x_in, cap_in, c_g, win_g, wout_g, x_g, wq_o, qkv, lse, att_o, ck_o, cv_o, e_o, vec,
                  q_g, n1, att, ckv, send, recv, local):
    at = position()
    partner = moved(at, "c", 1)
    row = [moved(at, "y", b) for b in (1, 3, 2)]
    greet([moved(at, a, b) for a in "zx" for b in (1, -1)] + row + [partner])
    copies = Copies(send, recv)
    me = (at["z"], at["x"], at["c"], at["y"])
    kept, sent = [], []

    def keep(src, dst):
        cp = pltpu.make_async_copy(src, dst, local.at[len(kept)])
        cp.start()
        kept.append(cp)

    keep(q_in.at[at["y"]], q_g.at[me])
    qx = [copies.start(q_in.at[to["y"]], q_g.at[me], to) for to in row]
    pairs = [copies.start(src, dst.at[me], partner) for src, dst in ((wout_in, wout_g), (win_in, win_g), (c_in, c_g))]
    for src, dst in ((wout_in, wout_g), (win_in, win_g), (c_in, c_g)):
        keep(src, dst.at[me])
    keep(x_in, x_g.at[at["y"]])
    keep(cap_in, e_o.at[:, quarter(at)])
    up, down = row[0], row[1]
    xx = [copies.start(x_in, x_g.at[at["y"]], to) for to in (up, down)]
    ee = [copies.start(cap_in, e_o.at[:, quarter(at)], to) for to in row]
    for s in kept + qx:
        s.wait()
    q_own = block(q_g, at, {"y"}, slice(None))
    qp = copies.start(q_own, q_own, partner)
    for s in pairs:
        s.wait()
    q_done, done = [], []
    fq = gather_flow(q_g, at, half(q_g.shape[-1], at), ("x", "z"), {"y", "c"}, copies, partner, q_done)
    fa = gather_flow(wout_g, at, half(1024, at), ("y", "z", "x"), {"c"}, copies, partner, done)
    fb = gather_flow(win_g, at, half(4096, at), ("x", "y", "z"), {"c"}, copies, partner, done)
    fc = gather_flow(c_g, at, half(c_g.shape[-1], at), ("z", "x", "y"), {"c"}, copies, partner, done)
    flows = [fa, fb, fc]
    for f in flows:
        next(f)
    qp.wait()
    next(fq)
    for s in xx:
        s.wait()
    low, high = slice(0, 128), slice(128, 256)
    x2 = [copies.start(x_g.at[down["y"], low], x_g.at[down["y"], low], up), copies.start(x_g.at[up["y"], high], x_g.at[up["y"], high], down)]
    for _ in range(4):
        next(fq, None)
        for f in flows:
            next(f)
    for s in x2 + ee + q_done:
        s.wait()

    wide = q_g[:, :, :, :, :, 1280:1408].astype(F32).reshape(1024, 128)
    vec[...] = wide.T[0:16, :]
    wq_o[...] = q_g[:, :, :, :, :, 0:1280].reshape(1024, 1280)
    x_rows = x_g.reshape(1024, 1024)
    project(x_rows, wq_o, vec, n1, qkv)
    ckv[...] = mm(e_o[...], wq_o[:, 768:1280]).astype(BF)
    self_forward(qkv, att, lse)
    for to in row:
        sent.append(copies.start(att.at[quarter(to)], att_o.at[:, quarter(at)], to))
        sent.append(copies.start(ckv.at[:, 0:256], ck_o.at[:, quarter(at)], to))
        sent.append(copies.start(ckv.at[:, 256:512], cv_o.at[:, quarter(at)], to))
    late = len(kept)
    keep(att.at[quarter(at)], att_o.at[:, quarter(at)])
    keep(ckv.at[:, 0:256], ck_o.at[:, quarter(at)])
    keep(ckv.at[:, 256:512], cv_o.at[:, quarter(at)])
    finish(flows)
    for s in sent + done + kept[late:]:
        s.wait()


def gathered(c_in, win_in, wout_in, q_in, x_in, cap_in):
    s = jax.ShapeDtypeStruct
    anywhere, vm = pl.BlockSpec(memory_space=pl.ANY), pl.BlockSpec(memory_space=pltpu.VMEM)
    outs = [s((4, 4, 2, 4, *a.shape), BF) for a in (c_in, win_in, wout_in)]
    outs += [s((4, 256, 1024), BF), s((1024, 1280), BF), s((1024, 768), BF), s((4, 1, 1024), F32), s((256, 1024), BF),
             s((128, 1024), BF), s((128, 1024), BF), s((128, 1024), BF), s((16, 1024), F32)]
    n = 100
    return pl.pallas_call(
        gather_kernel, out_shape=outs, in_specs=[anywhere] * 6, out_specs=[anywhere] * 3 + [vm] * 9,
        scratch_shapes=[pltpu.VMEM((4, 4, 2, 4, *q_in.shape[1:]), BF), pltpu.VMEM((1024, 1024), BF), pltpu.VMEM((1024, 256), BF),
                        pltpu.VMEM((128, 512), BF), pltpu.SemaphoreType.DMA((n,)), pltpu.SemaphoreType.DMA((n,)), pltpu.SemaphoreType.DMA((10,))],
        compiler_params=pltpu.CompilerParams(collective_id=0, has_side_effects=True, vmem_limit_bytes=60 << 20),
        name="gather_and_attend",
    )(c_in, win_in, wout_in, q_in, x_in, cap_in)


ORDER = ("z", "x", "c", "y")
def part(ref, at, whole, **fixed):
    return ref.at[tuple(fixed[a] if a in fixed else slice(None) if a in whole else at[a] for a in ORDER)]


def each(shape, body):
    total = 1
    for s in shape:
        total *= s

    def step(i, _):
        index, rest = [], i
        for s in reversed(shape):
            index.insert(0, lax.rem(rest, s))
            rest = lax.div(rest, s)
        body(tuple(index))
        return 0

    if total == 1:
        body((0,) * len(shape))
    else:
        lax.fori_loop(0, total, step, 0)


def add_into(dst, *srcs):
    def one(index):
        total = dst[index].astype(jnp.float32)
        for s in srcs:
            total += s[index].astype(jnp.float32)
        dst[index] = total.astype(dst.dtype)

    each(dst.shape[:-2], one)


def landing_shapes(lead, rows, cols, axes):
    whole = {"z", "x", "y"} & set(lead)
    shapes = []
    for axis in axes:
        whole = whole - {axis}
        dims = tuple(4 for a in ("z", "x", "y") if a in whole)
        shapes.append((6, *dims, rows, cols))
    return shapes


def scatter_flow(g, landing, at, axes, whole, copies):
    whole = set(whole)
    for axis, land in zip(axes, landing):
        up, down, far = moved(at, axis, 1), moved(at, axis, -1), moved(at, axis, 2)
        rest = whole - {axis}
        def blk(place, core):
            return part(g, at, rest, **{axis: place[axis], "c": core})
        s = [
            copies.start(blk(far, 0), land.at[0], up),
            copies.start(blk(far, 1), land.at[1], down),
            copies.start(blk(up, 1), land.at[2], up),
            copies.start(blk(down, 0), land.at[3], down),
        ]
        yield
        s[0].wait_recv()
        add_into(blk(up, 0), land.at[0])
        s.append(copies.start(blk(up, 0), land.at[4], up))
        s[1].wait_recv()
        add_into(blk(down, 1), land.at[1])
        s.append(copies.start(blk(down, 1), land.at[5], down))
        yield
        s[2].wait_recv()
        s[5].wait_recv()
        add_into(blk(at, 1), land.at[2], land.at[5])
        s[3].wait_recv()
        s[4].wait_recv()
        add_into(blk(at, 0), land.at[3], land.at[4])
        for q in s:
            q.wait_send()
        whole = rest


def reduce_kernel(u, dy, n3, dh, att, r1, n2, dcq, catt, r2, datt, dckv, vec_sums, x_all, qkv, lse, wq, e, dx1, vec,
                  out_a, out_b, out_c, out_q, tok, cap,
                  u2, dy2, n32, dh2, a2, r2s, ga, gb, gc, gq, gql, datt4, dckv4, dcap, dcap4, dqkv, n1, dk, dv, dn, dn4, v13,
                  la1, la2, la3, lb1, lb2, lb3, lc1, lc2, lc3, lq1, lq2, fa, fb, fc, fq, send, recv, local):
    at = position()
    partner = moved(at, "c", 1)
    row = [moved(at, "y", b) for b in (1, 3, 2)]
    ring = row + [moved(o, "c", 1) for o in row] + [partner]
    greet([moved(at, a, b) for a in "zx" for b in (1, -1)] + ring)
    copies = Copies(send, recv)
    c, y = at["c"], at["y"]
    loads, pairs = [], []

    def both(src, dst, split):
        n = src.shape[-1]
        rows = src.shape[0]
        mine = src.at[:, half(n, at)] if split else src
        theirs = src.at[:, half(n, partner)] if split else src
        cp = pltpu.make_async_copy(mine, dst.at[pl.ds(0, rows)], local.at[len(loads)])
        cp.start()
        loads.append(cp)
        pairs.append(copies.start(theirs, dst.at[pl.ds(rows, rows)], partner))
        return len(loads) - 1

    def ready(*ks):
        for k in ks:
            loads[k].wait()
            pairs[k].wait()

    kb = [both(n3, n32, False), both(dh, dh2, True)]
    own_rows = pl.ds(pl.multiple_of(y * 256, 256), 256)
    d_own = pltpu.make_async_copy(datt.at[:, quarter(at)], datt4.at[own_rows], local.at[30])
    d_own.start()
    dd = [copies.start(datt.at[:, quarter(to)], datt4.at[own_rows], to) for to in row]
    kv_own = [pltpu.make_async_copy(dckv.at[:, pl.ds(pl.multiple_of(k * 1024 + y * 256, 256), 256)], dckv4.at[y, :, pl.ds(k * 256, 256)], local.at[28 + k]) for k in range(2)]
    for s in kv_own:
        s.start()
    kvs = [copies.start(dckv.at[:, pl.ds(pl.multiple_of(k * 1024 + to["y"] * 256, 256), 256)], dckv4.at[y, :, pl.ds(k * 256, 256)], to)
           for to in row for k in range(2)]
    ka = [both(u, u2, False), both(dy, dy2, True)]
    kc = []
    for k, (a, b) in enumerate(((att, r1), (n2, dcq), (catt, r2))):
        kc += [both(a, a2.at[k], False), both(b, r2s.at[k], True)]

    def grad_b(z):
        lhs = n32[:, pl.ds(pl.multiple_of(z * 256, 256), 256)]
        for k in range(4):
            g = mm_rows(lhs, dh2[:, k * 512:(k + 1) * 512])
            gb[z, :, :, :, :, k * 512:(k + 1) * 512] = g.reshape(4, 2, 4, 8, 512).astype(BF)

    def grad_a(z, x):
        lhs = u2[:, pl.ds(pl.multiple_of((z * 4 + x) * 256, 256), 256)]
        ga[z, x] = mm_rows(lhs, dy2[...]).reshape(2, 4, 32, 512).astype(BF)

    def grad_c(k, z):
        g = mm_rows(a2[k, :, pl.ds(pl.multiple_of(z * 256, 256), 256)], r2s[k])
        gc[z, :, :, :, :, k * 512:(k + 1) * 512] = g.reshape(4, 2, 4, 8, 512).astype(BF)

    ready(*kb)
    far_z, far_x = moved(at, "z", 2)["z"], moved(at, "x", 2)["x"]
    loop(4, lambda i: grad_b(lax.rem(far_z + i, 4)))
    fl_b = scatter_flow(gb, (lb1, lb2, lb3), at, ("z", "y", "x"), {"z", "x", "y"}, copies)
    next(fl_b)
    ready(*ka)
    loop(16, lambda i: grad_a(lax.rem(i, 4), lax.rem(far_x + lax.div(i, 4), 4)))
    fl_a = scatter_flow(ga, (la1, la2, la3), at, ("x", "z", "y"), {"z", "x", "y"}, copies)
    next(fl_a)
    ready(*kc)
    for k in range(3):
        loop(4, functools.partial(grad_c, k))
    fl_c = scatter_flow(gc, (lc1, lc2, lc3), at, ("y", "x", "z"), {"z", "x", "y"}, copies)
    next(fl_c)

    for s in kv_own + kvs:
        s.wait()
    dckv4[0] = sum(dckv4[k].astype(F32) for k in range(4)).astype(BF)
    dcap[...] = mm_cols(dckv4[0], wq[:, 768:1280]).astype(BF)
    cap_own = pltpu.make_async_copy(dcap.at[:, quarter(at)], dcap4.at[y], local.at[27])
    cap_own.start()
    caps = [copies.start(dcap.at[:, quarter(to)], dcap4.at[y], to) for to in row]

    d_own.wait()
    for s in dd:
        s.wait()
    self_backward(qkv, lse, datt4, dqkv, dk, dv)
    v13[...] = vec_sums[...]
    gain, shift = vec[0:1, :], vec[3:4, :]

    def norm_rows(i):
        r = pl.ds(pl.multiple_of(i * 128, 128), 128)
        z, _ = normed(x_all[r, :].astype(F32))
        n1[r, :] = (z * gain + shift).astype(BF)
        d = mm_cols(dqkv[r, :], wq[:, 0:768])
        dn[r, :] = d.astype(BF)
        v13[0:1, :] += jnp.sum(d * z, axis=0, keepdims=True)
        v13[3:4, :] += jnp.sum(d, axis=0, keepdims=True)

    loop(8, norm_rows)
    dns = [copies.start(dn.at[pl.ds(pl.multiple_of(to["y"] * 256, 256), 256)], dn4.at[k], to) for k, to in enumerate(row)]

    def grad_q(z):
        cols = pl.ds(pl.multiple_of(z * 256, 256), 256)
        gq[z, :, :, :, :, 0:768] = mm_rows(n1[:, cols], dqkv[...]).reshape(4, 2, 4, 8, 768).astype(BF)
        gq[z, :, :, :, :, 768:1280] = mm_rows(e[:, cols], dckv4[0]).reshape(4, 2, 4, 8, 512).astype(BF)

    loop(4, grad_q)
    gq[:, :, :, :, :, 1280:1408] = v13[...].T.reshape(4, 4, 2, 4, 8, 128).astype(BF)
    gq[:, :, :, :, :, 1408:1536] = jnp.zeros((4, 4, 2, 4, 8, 128), BF)
    n_q = gq.shape[-1]
    pq = copies.start(gq.at[:, :, :, :, :, half(n_q, partner)], gql, partner)
    flows = [fl_b, fl_a, fl_c]
    for f in flows:
        next(f)
    pq.wait()
    mine = gq.at[:, :, :, :, :, half(n_q, at)]
    add_into(mine, gql)
    fl_q = scatter_flow(mine, (lq1, lq2), at, ("x", "z"), {"z", "x", "y"}, copies)
    next(fl_q)
    for f in flows:
        next(f)
    next(fl_q)
    for s in dns + caps + [cap_own]:
        s.wait()

    def token_rows(i):
        r = pl.ds(pl.multiple_of(i * 64, 64), 64)
        here = pl.ds(pl.multiple_of(y * 256 + i * 64, 64), 64)
        d = dn[here, :].astype(F32) + dn4[0, r, :].astype(F32) + dn4[1, r, :].astype(F32) + dn4[2, r, :].astype(F32)
        back, _, _ = norm_back(x_all[here, :].astype(F32), d, gain)
        tok[r, :] = dx1[r, :] + back

    loop(4, token_rows)
    cap[...] = sum(dcap4[k].astype(F32) for k in range(4))
    finish(flows + [fl_q])

    last = []
    for g, f in ((ga, fa), (gb, fb), (gc, fc)):
        last.append(copies.start(g.at[at["z"], at["x"], partner["c"], y], f, partner))
    for o in ring:
        last.append(copies.start(mine.at[at["z"], at["x"], o["c"], o["y"]], fq.at[c, y], o))
    own_q = pltpu.make_async_copy(mine.at[at["z"], at["x"], c, y], fq.at[c, y], local.at[26])
    own_q.start()
    for g, o in ((ga, out_a), (gb, out_b), (gc, out_c)):
        o[c] = g[at["z"], at["x"], c, y].astype(F32)
    for s in last + [own_q]:
        s.wait()
    for f, o in ((fa, out_a), (fb, out_b), (fc, out_c)):
        o[partner["c"]] = f[...].astype(F32)
    out_q[...] = fq[...].astype(F32)


def reduced(u, dy, n3, dh, att, r1, n2, dcq, catt, r2, datt, dckv, vec_sums, x_all, qkv, lse, wq, e, dx1, vec):
    n_c, n_q = 1536, 768
    lead = ("z", "x", "y")
    V = pltpu.VMEM
    scratch = [
        V((512, 4096), BF), V((512, 512), BF), V((512, 1024), BF), V((512, 2048), BF), V((3, 512, 1024), BF), V((3, 512, 512), BF),
        V((4, 4, 2, 4, 32, 512), BF), V((4, 4, 2, 4, 8, 2048), BF), V((4, 4, 2, 4, 8, n_c), BF),
        V((4, 4, 2, 4, 8, 2 * n_q), BF), V((4, 4, 2, 4, 8, n_q), BF),
        V((1024, 256), BF), V((4, 128, 512), BF), V((128, 1024), BF), V((4, 128, 256), BF), V((1024, 768), BF), V((1024, 1024), BF),
        V((1024, 128), F32), V((1024, 128), F32), V((1024, 1024), BF), V((3, 256, 1024), BF), V((128, 1024), F32),
    ]
    for r, n, axes in ((32, 512, "xzy"), (8, 2048, "zyx"), (8, n_c, "yxz"), (8, n_q, "xz")):
        scratch += [V(s, BF) for s in landing_shapes(lead, r, n, axes)]
    scratch += [V((32, 512), BF), V((8, 2048), BF), V((8, n_c), BF), V((2, 4, 8, n_q), BF)]
    n = 112
    scratch += [pltpu.SemaphoreType.DMA((n,)), pltpu.SemaphoreType.DMA((n,)), pltpu.SemaphoreType.DMA((32,))]
    s = jax.ShapeDtypeStruct
    outs = [s((2, 32, 512), F32), s((2, 8, 2048), F32), s((2, 8, n_c), F32), s((2, 4, 8, n_q), F32), s((256, 1024), F32), s((128, 256), F32)]
    anywhere, vm = pl.BlockSpec(memory_space=pl.ANY), pl.BlockSpec(memory_space=pltpu.VMEM)
    return pl.pallas_call(
        reduce_kernel, out_shape=outs, in_specs=[anywhere] * 12 + [vm] * 8, out_specs=[vm] * 6,
        scratch_shapes=scratch,
        compiler_params=pltpu.CompilerParams(collective_id=1, has_side_effects=True, vmem_limit_bytes=62 << 20),
        name="reduce_gradients",
    )(u, dy, n3, dh, att, r1, n2, dcq, catt, r2, datt, dckv, vec_sums, x_all, qkv, lse, wq, e, dx1, vec)


def local(tokens, captions, cap_lengths, w_qkv, w_self_out, w_cross_q, w_cross_kv, w_cross_out, w_in, w_out,
          norm_gains, norm_shifts, out_biases, in_bias, out_grad):
    vectors = jnp.concatenate([norm_gains.T, norm_shifts.T, out_biases.T, in_bias.reshape(4, 8).T], axis=1)
    vectors = jnp.pad(vectors, ((0, 0), (0, 256 - 13)))
    c_in = jnp.concatenate([w_self_out, w_cross_q, w_cross_out], axis=1)
    q_in = jnp.concatenate([w_qkv, w_cross_kv], axis=1).reshape(8, 5, 4, 256).transpose(2, 0, 1, 3).reshape(4, 8, 1280)
    q_in = jnp.concatenate([q_in, jnp.broadcast_to(vectors, (4, 8, 256))], axis=2)
    c_g, win_g, wout_g, x_g, wq, qkv, lse, att, ck, cv, e, vec = gathered(c_in, w_in, w_out, q_in, tokens[0], captions[0])
    wc, full_in, full_out = c_g.reshape(1024, -1), win_g.reshape(1024, -1), wout_g.reshape(4096, 1024)
    hidden_bias = vec[9:13].reshape(4, 128, 8).transpose(1, 0, 2).reshape(1, 4096)
    dy = out_grad[0]
    (layer_out, dx1, datt, dckv, n2, n3, catt, u, dh, r1, r2, dcq, sums, d_in_bias) = middle(
        cap_lengths, tokens[0], att, dy, ck, cv, vec, hidden_bias, wc, full_in, full_out)
    d_hidden = d_in_bias.reshape(128, 4, 8).transpose(1, 0, 2).reshape(4, 1024)
    vec_sums = jnp.concatenate([sums[:9], d_hidden, jnp.zeros((115, 1024), jnp.float32)], axis=0)
    out_a, out_b, out_c, out_q, tokens_grad, captions_grad = reduced(
        u, dy, n3, dh, att, r1, n2, dcq, catt, r2, datt, dckv, vec_sums, x_g.reshape(1024, 1024), qkv, lse, wq, e, dx1, vec)
    joined = lambda t: jnp.concatenate([t[0], t[1]], axis=1)
    q_out = out_q.transpose(2, 1, 0, 3).reshape(8, 4, 1536)
    vec_out = q_out[:, :, 1280:1293].sum(axis=1)
    q_out = q_out[:, :, :1280].reshape(8, 4, 5, 256).transpose(0, 2, 1, 3).reshape(8, 5120)
    return (
        layer_out[None], tokens_grad[None], captions_grad[None],
        q_out[:, :3072], joined(out_c[..., :512]), joined(out_c[..., 512:1024]), q_out[:, 3072:], joined(out_c[..., 1024:1536]),
        joined(out_b), joined(out_a), vec_out[:, :3].T, vec_out[:, 3:6].T, vec_out[:, 6:9].T, vec_out[:, 9:13].T.reshape(32),
    )


def solution(mesh):
    rows, tokens, vectors = P(("dp", "seq"), None), P("dp", "seq", None), P(None, ("dp", "seq"))
    captions = P("dp", None, "seq")
    return jax.shard_map(
        local, mesh=mesh,
        in_specs=(tokens, captions, P("dp"), *[rows] * 7, *[vectors] * 3, P(("dp", "seq")), tokens),
        out_specs=(tokens, tokens, captions, *[rows] * 7, *[vectors] * 3, P(("dp", "seq"))),
        check_vma=False,
    )
```

profile of v0, /device:TPU:1, one launch (start us, length us, event | category | flops | bytes accessed | tf_op | source)
XLA Modules:
  0.0 259.2 jit_solution(12052007878809347528)
XLA Ops:
  0.6 0.8 pad_maximum_fusion.3
  1.5 0.7 reshape.75
  2.2 0.7 pad_maximum_fusion.8
  2.9 0.1 copy.54
  3.1 0.6 pad_maximum_fusion.2.q_in
  3.7 1.4 pad_maximum_fusion.4.c_in
  5.1 94.9 %gather_and_attend.1 = (bf16[4,4,2,4,8,3072]{5,4,3,2,1,0:T(8,128)(2,1)}, bf16[4,4,2,4,8,4096]{5,4,3,2,1,0:T(8,128)(2,1)}, bf16[4,4,2,4,32,1024]{5,4,3,2,1,0:T(8,...) custom-call(bf16[8,3072]{1,0:T(8,128)(2,1)} %pad_maximum_fusion.4.c_, ...), custom_call_target="tpu_custom_call" | custom-call | tf_op jit(solution)/shard_map/gather_and_attend/pallas_call | solution.py:446
  100.0 0.8 slice.69
  100.8 0.2 reshape.76
  101.0 0.2 copy.46
  101.1 0.9 reshape.77.inb
  102.7 38.2 %middle.1 = (bf16[256,1024]{1,0:T(8,128)(2,1)}, f32[256,1024]{1,0:T(8,128)}, bf16[256,1024]{1,0:T(8,128)(2,1)}, bf16[128,2048]{1,0:T(8,128)(2,1)}, bf16[256,1024...) custom-call(s32[1]{0:T(128)S(6)} %copy.58.length, ...), custom_call_target="tpu_custom_call" | custom-call | tf_op jit(solution)/shard_map/middle/pallas_call | solution.py:267
  140.8 0.5 broadcast.7
  141.3 1.4 reduce.3
  142.7 0.3 reshape.81
  143.1 0.2 reshape.82
  143.3 0.1 pad.17.clone
  143.4 1.8 maximum_maximum_fusion.vec_sums
  145.1 101.8 %reduce_gradients.1 = (f32[2,32,512]{2,1,0:T(8,128)}, f32[2,8,2048]{2,1,0:T(8,128)}, f32[2,8,1536]{2,1,0:T(8,128)}, f32[2,4,8,768]{3,2,1,0:T(8,128)}, f32[256,1024]{1,0:T(8,128)}, /*index=5*/f32[128,256]{1,0:T(8,128)}) custom-call(bf16[256,4096]{1,0:T(8,128)(2,1)} %get-tuple-element.54.u, bf16[256,1024]{1,0:T(8,128)(2,1)} %bitcast.60, ...), custom_call_target="tpu_custom_call" | custom-call | tf_op jit(solution)/shard_map/reduce_gradients/pallas_call | solution.py:701
  247.0 0.0 copy-start
  247.0 1.0 slice_bitcast_fusion.1
  247.9 0.7 pad_maximum_fusion.1
  248.6 0.0 copy-start.1
  248.6 0.9 slice_bitcast_fusion.3
  249.5 0.7 pad_maximum_fusion
  250.2 0.8 slice_bitcast_fusion.5
  251.0 0.6 pad_maximum_fusion.7
  251.6 0.6 pad_maximum_fusion.5
  252.3 0.9 copy.55
  253.3 0.1 copy.49
  253.4 0.1 reshape.86
  253.5 0.6 slice.90
  254.1 0.6 slice.91
  254.8 0.1 slice_bitcast_fusion.11
  254.8 0.7 copy.51
  255.5 0.7 copy.52
  256.2 0.7 copy.53
  256.8 0.1 slice_bitcast_fusion.10
  256.9 0.1 copy.50
  257.0 0.6 reshape.87
  257.6 0.0 copy-done
  257.6 1.0 copy.59
  258.5 0.0 copy-done.1
  258.5 0.7 copy.60
  (8 shorter events, 0.1 us)
Async XLA Ops:
  247.0 10.6 %copy-start = (f32[256,1024]{1,0:T(8,128)S(1)}, f32[256,1024]{1,0:T(8,128)}, u32[]{:S(2)}) copy-start(f32[256,1024]{1,0:T(8,128)} %get-tuple-element.72) | copy-start | bytes 3145732
  248.6 9.9 %copy-start.1 = (f32[128,256]{1,0:T(8,128)S(1)}, f32[128,256]{1,0:T(8,128)}, u32[]{:S(2)}) copy-start(f32[128,256]{1,0:T(8,128)} %get-tuple-element.73) | copy-start | bytes 393220
where the time goes:
time: 260 us; the launch traced here: 259 us
  Pallas kernels  235 us (90%)
  local copies, waits for them, and re-layouts  13.5 us (5%)
  other arithmetic  9.31 us (4%)
    pallas_call x1, Pallas kernels, reduced(): pl.pallas_call(reduce_kernel, out_shape=outs, in_specs=[anywhere] * 12 +...  102 us
    pallas_call x1, Pallas kernels, gathered(): pl.pallas_call(gather_kernel, out_shape=outs, in_specs=[anywhere] * 6, ou...  94.9 us
    pallas_call x1, Pallas kernels, middle(): pl.pallas_call(middle_kernel, out_shape=outs, in_specs=[pl.BlockSpec(memo...  38.2 us

commit v1 on v0

--- a/solution.py
+++ b/solution.py
@@ -29,30 +29,33 @@
     def start(self, src, dst, at):
         k = self.used
         self.used += 1
+        assert k < self.send.shape[0]
         copy = pltpu.make_async_remote_copy(src_ref=src, dst_ref=dst, send_sem=self.send.at[k], recv_sem=self.recv.at[k], device_id=device(at), device_id_type=MESH)
         copy.start()
         return copy
 
 
-def block(ref, at, whole, cols, **fixed):
-    idx = []
-    for axis in ("z", "x", "c", "y"):
-        idx.append(fixed[axis] if axis in fixed else slice(None) if axis in whole else at[axis])
+def block(ref, at, whole, cols):
+    idx = [slice(None) if axis in whole else at[axis] for axis in ("z", "x", "c", "y")]
     return ref.at[(*idx, slice(None), cols)]
 
 
-def gather_flow(ref, at, cols, axes, whole, copies, partner, done):
+def gather_flow(ref, at, cols, axes, whole, copies, partner, done, source=None):
+    start, size = cols
+    low_cols, high_cols = pl.ds(start, size // 256 * 128), pl.ds(start + size // 256 * 128, size - size // 256 * 128)
+    cols = pl.ds(start, size)
     whole = set(whole)
     for axis in axes:
         up, down = moved(at, axis, 1), moved(at, axis, -1)
         own = block(ref, at, whole, cols)
-        a = copies.start(own, own, up)
-        b = copies.start(own, own, down)
+        src = own if source is None else source.at[:, cols]
+        source = None
+        a = copies.start(src, own, up)
+        b = copies.start(src, own, down)
         yield
         a.wait_recv()
         b.wait_recv()
-        low = block(ref, down, whole, cols, c=0)
-        high = block(ref, up, whole, cols, c=1)
+        low, high = block(ref, down, whole, low_cols), block(ref, up, whole, high_cols)
         c = copies.start(low, low, up)
         d = copies.start(high, high, down)
         for p in (down, up):
@@ -314,9 +317,9 @@
     loop(2, pair)
 
 
-def self_backward(qkv, lse, datt, dqkv, dk, dv):
+def self_backward(p, qkv, lse, datt, dqkv, dk, dv):
     def pair(p):
-        at = lambda part: pl.ds(pl.multiple_of(part * 256 + p * 128, 128), 128)
+        at = lambda part: pl.ds(part * 256 + p * 128, 128)
         dk[...] = jnp.zeros_like(dk)
         dv[...] = jnp.zeros_like(dv)
         for i in range(1024 // BLOCK):
@@ -338,7 +341,7 @@
         dqkv[:, at(1)] = (dk[...] * SCALE).astype(BF)
         dqkv[:, at(2)] = dv[...].astype(BF)
 
-    loop(2, pair)
+    pair(p)
 
 
 def greet(others):
@@ -381,38 +384,43 @@
 
     keep(q_in.at[at["y"]], q_g.at[me])
     qx = [copies.start(q_in.at[to["y"]], q_g.at[me], to) for to in row]
-    pairs = [copies.start(src, dst.at[me], partner) for src, dst in ((wout_in, wout_g), (win_in, win_g), (c_in, c_g))]
+    q_done, done = [], []
+    flows = []
+    for src, dst, axes, st, n in ((wout_in, wout_g, "yzx", 0, 512), (win_in, win_g, "yxz", 0, 2048), (c_in, c_g, "xzy", 0, 1536),
+                                  (wout_in, wout_g, "yzx", 512, 512), (win_in, win_g, "yxz", 2048, 2048), (c_in, c_g, "zxy", 1536, 1536)):
+        flows.append(gather_flow(dst, at, (st, n), axes, (), copies, partner, done, src))
+    for f in flows:
+        next(f)
+    keep(x_in, x_g.at[at["y"]])
+    up, down = row[0], row[1]
+    keep(cap_in, e_o.at[:, quarter(at)])
+    ee = [copies.start(cap_in, e_o.at[:, quarter(at)], to) for to in row]
     for src, dst in ((wout_in, wout_g), (win_in, win_g), (c_in, c_g)):
         keep(src, dst.at[me])
-    keep(x_in, x_g.at[at["y"]])
-    keep(cap_in, e_o.at[:, quarter(at)])
-    up, down = row[0], row[1]
-    xx = [copies.start(x_in, x_g.at[at["y"]], to) for to in (up, down)]
-    ee = [copies.start(cap_in, e_o.at[:, quarter(at)], to) for to in row]
-    for s in kept + qx:
+        done.append(copies.start(src, dst.at[me], partner))
+    for s in [kept[0]] + qx:
         s.wait()
     q_own = block(q_g, at, {"y"}, slice(None))
-    qp = copies.start(q_own, q_own, partner)
-    for s in pairs:
+    q_done.append(copies.start(q_own, q_own, partner))
+    fq = [gather_flow(q_g, at, (0, 640), "zx", {"y"}, copies, partner, q_done),
+          gather_flow(q_g, at, (640, 768), "xz", {"y"}, copies, partner, q_done)]
+    for f in fq:
+        next(f)
+    for s in kept[1:]:
         s.wait()
-    q_done, done = [], []
-    fq = gather_flow(q_g, at, half(q_g.shape[-1], at), ("x", "z"), {"y", "c"}, copies, partner, q_done)
-    fa = gather_flow(wout_g, at, half(1024, at), ("y", "z", "x"), {"c"}, copies, partner, done)
-    fb = gather_flow(win_g, at, half(4096, at), ("x", "y", "z"), {"c"}, copies, partner, done)
-    fc = gather_flow(c_g, at, half(c_g.shape[-1], at), ("z", "x", "y"), {"c"}, copies, partner, done)
-    flows = [fa, fb, fc]
-    for f in flows:
-        next(f)
-    qp.wait()
-    next(fq)
-    for s in xx:
-        s.wait()
-    low, high = slice(0, 128), slice(128, 256)
-    x2 = [copies.start(x_g.at[down["y"], low], x_g.at[down["y"], low], up), copies.start(x_g.at[up["y"], high], x_g.at[up["y"], high], down)]
-    for _ in range(4):
-        next(fq, None)
+    for k in range(4):
+        for f in fq:
+            next(f, None)
         for f in flows:
             next(f)
+        if k == 0:
+            xx = [copies.start(x_in, x_g.at[at["y"]], to) for to in (up, down)]
+        if k == 1:
+            for s in xx:
+                s.wait()
+            low, high = slice(0, 128), slice(128, 256)
+            x2 = [copies.start(x_g.at[down["y"], low], x_g.at[down["y"], low], up),
+                  copies.start(x_g.at[up["y"], high], x_g.at[up["y"], high], down)]
     for s in x2 + ee + q_done:
         s.wait()
 
@@ -442,7 +450,7 @@
     outs = [s((4, 4, 2, 4, *a.shape), BF) for a in (c_in, win_in, wout_in)]
     outs += [s((4, 256, 1024), BF), s((1024, 1280), BF), s((1024, 768), BF), s((4, 1, 1024), F32), s((256, 1024), BF),
              s((128, 1024), BF), s((128, 1024), BF), s((128, 1024), BF), s((16, 1024), F32)]
-    n = 100
+    n = 196
     return pl.pallas_call(
         gather_kernel, out_shape=outs, in_specs=[anywhere] * 6, out_specs=[anywhere] * 3 + [vm] * 9,
         scratch_shapes=[pltpu.VMEM((4, 4, 2, 4, *q_in.shape[1:]), BF), pltpu.VMEM((1024, 1024), BF), pltpu.VMEM((1024, 256), BF),
@@ -486,14 +494,12 @@
     each(dst.shape[:-2], one)
 
 
-def landing_shapes(lead, rows, cols, axes):
-    whole = {"z", "x", "y"} & set(lead)
-    shapes = []
+def landing_shapes(rows, cols, axes):
+    whole, shapes = {"z", "x", "y"}, []
     for axis in axes:
         whole = whole - {axis}
-        dims = tuple(4 for a in ("z", "x", "y") if a in whole)
-        shapes.append((6, *dims, rows, cols))
-    return shapes
+        shapes.append(pltpu.VMEM((6, *[4 for a in ("z", "x", "y") if a in whole], rows, cols), jnp.bfloat16))
+    return tuple(shapes)
 
 
 def scatter_flow(g, landing, at, axes, whole, copies):
@@ -531,7 +537,7 @@
 def reduce_kernel(u, dy, n3, dh, att, r1, n2, dcq, catt, r2, datt, dckv, vec_sums, x_all, qkv, lse, wq, e, dx1, vec,
                   out_a, out_b, out_c, out_q, tok, cap,
                   u2, dy2, n32, dh2, a2, r2s, ga, gb, gc, gq, gql, datt4, dckv4, dcap, dcap4, dqkv, n1, dk, dv, dn, dn4, v13,
-                  la1, la2, la3, lb1, lb2, lb3, lc1, lc2, lc3, lq1, lq2, fa, fb, fc, fq, send, recv, local):
+                  la, lb, lc0, lc1, lc2, lq0, lq1, fa, fb, fc, fq, send, recv, local):
     at = position()
     partner = moved(at, "c", 1)
     row = [moved(at, "y", b) for b in (1, 3, 2)]
@@ -586,20 +592,21 @@
         g = mm_rows(a2[k, :, pl.ds(pl.multiple_of(z * 256, 256), 256)], r2s[k])
         gc[z, :, :, :, :, k * 512:(k + 1) * 512] = g.reshape(4, 2, 4, 8, 512).astype(BF)
 
+    every = {"z", "x", "y"}
     ready(*kb)
-    far_z, far_x = moved(at, "z", 2)["z"], moved(at, "x", 2)["x"]
-    loop(4, lambda i: grad_b(lax.rem(far_z + i, 4)))
-    fl_b = scatter_flow(gb, (lb1, lb2, lb3), at, ("z", "y", "x"), {"z", "x", "y"}, copies)
+    loop(4, grad_b)
+    fl_b = scatter_flow(gb, lb, at, ("z", "x", "y"), every, copies)
     next(fl_b)
     ready(*ka)
-    loop(16, lambda i: grad_a(lax.rem(i, 4), lax.rem(far_x + lax.div(i, 4), 4)))
-    fl_a = scatter_flow(ga, (la1, la2, la3), at, ("x", "z", "y"), {"z", "x", "y"}, copies)
+    loop(16, lambda i: grad_a(lax.rem(i, 4), lax.div(i, 4)))
+    fl_a = scatter_flow(ga, la, at, ("x", "z", "y"), every, copies)
     next(fl_a)
     ready(*kc)
-    for k in range(3):
+    fl_c = []
+    for k, (land, axes) in enumerate(((lc0, "yzx"), (lc1, "zyx"), (lc2, "yzx"))):
         loop(4, functools.partial(grad_c, k))
-    fl_c = scatter_flow(gc, (lc1, lc2, lc3), at, ("y", "x", "z"), {"z", "x", "y"}, copies)
-    next(fl_c)
+        fl_c.append(scatter_flow(gc.at[:, :, :, :, :, pl.ds(k * 512, 512)], land, at, tuple(axes), every, copies))
+        next(fl_c[k])
 
     for s in kv_own + kvs:
         s.wait()
@@ -612,7 +619,10 @@
     d_own.wait()
     for s in dd:
         s.wait()
-    self_backward(qkv, lse, datt4, dqkv, dk, dv)
+    self_backward(0, qkv, lse, datt4, dqkv, dk, dv)
+    self_backward(1, qkv, lse, datt4, dqkv, dk, dv)
+    next(fl_b)
+    next(fl_a)
     v13[...] = vec_sums[...]
     gain, shift = vec[0:1, :], vec[3:4, :]
 
@@ -627,6 +637,8 @@
 
     loop(8, norm_rows)
     dns = [copies.start(dn.at[pl.ds(pl.multiple_of(to["y"] * 256, 256), 256)], dn4.at[k], to) for k, to in enumerate(row)]
+    for f in fl_c:
+        next(f)
 
     def grad_q(z):
         cols = pl.ds(pl.multiple_of(z * 256, 256), 256)
@@ -638,17 +650,15 @@
     gq[:, :, :, :, :, 1408:1536] = jnp.zeros((4, 4, 2, 4, 8, 128), BF)
     n_q = gq.shape[-1]
     pq = copies.start(gq.at[:, :, :, :, :, half(n_q, partner)], gql, partner)
-    flows = [fl_b, fl_a, fl_c]
-    for f in flows:
-        next(f)
+    next(fl_b)
+    next(fl_a)
     pq.wait()
     mine = gq.at[:, :, :, :, :, half(n_q, at)]
     add_into(mine, gql)
-    fl_q = scatter_flow(mine, (lq1, lq2), at, ("x", "z"), {"z", "x", "y"}, copies)
-    next(fl_q)
-    for f in flows:
+    q_cols = lambda k: gq.at[:, :, :, :, :, pl.ds(pl.multiple_of(c * 768 + k * 384, 128), 384)]
+    fl_q = [scatter_flow(q_cols(0), lq0, at, ("x", "z"), every, copies), scatter_flow(q_cols(1), lq1, at, ("z", "x"), every, copies)]
+    for f in fl_q + fl_c + [fl_b, fl_a] + fl_q:
         next(f)
-    next(fl_q)
     for s in dns + caps + [cap_own]:
         s.wait()
 
@@ -661,7 +671,7 @@
 
     loop(4, token_rows)
     cap[...] = sum(dcap4[k].astype(F32) for k in range(4))
-    finish(flows + [fl_q])
+    finish(fl_c + [fl_b, fl_a] + fl_q)
 
     last = []
     for g, f in ((ga, fa), (gb, fb), (gc, fc)):
@@ -671,17 +681,16 @@
     own_q = pltpu.make_async_copy(mine.at[at["z"], at["x"], c, y], fq.at[c, y], local.at[26])
     own_q.start()
     for g, o in ((ga, out_a), (gb, out_b), (gc, out_c)):
-        o[c] = g[at["z"], at["x"], c, y].astype(F32)
+        o[c] = g[at["z"], at["x"], c, y]
     for s in last + [own_q]:
         s.wait()
     for f, o in ((fa, out_a), (fb, out_b), (fc, out_c)):
-        o[partner["c"]] = f[...].astype(F32)
-    out_q[...] = fq[...].astype(F32)
+        o[partner["c"]] = f[...]
+    out_q[...] = fq[...]
 
 
 def reduced(u, dy, n3, dh, att, r1, n2, dcq, catt, r2, datt, dckv, vec_sums, x_all, qkv, lse, wq, e, dx1, vec):
     n_c, n_q = 1536, 768
-    lead = ("z", "x", "y")
     V = pltpu.VMEM
     scratch = [
         V((512, 4096), BF), V((512, 512), BF), V((512, 1024), BF), V((512, 2048), BF), V((3, 512, 1024), BF), V((3, 512, 512), BF),
@@ -690,13 +699,13 @@
         V((1024, 256), BF), V((4, 128, 512), BF), V((128, 1024), BF), V((4, 128, 256), BF), V((1024, 768), BF), V((1024, 1024), BF),
         V((1024, 128), F32), V((1024, 128), F32), V((1024, 1024), BF), V((3, 256, 1024), BF), V((128, 1024), F32),
     ]
-    for r, n, axes in ((32, 512, "xzy"), (8, 2048, "zyx"), (8, n_c, "yxz"), (8, n_q, "xz")):
-        scratch += [V(s, BF) for s in landing_shapes(lead, r, n, axes)]
+    scratch += [landing_shapes(32, 512, "xzy"), landing_shapes(8, 2048, "zxy")]
+    scratch += [landing_shapes(8, 512, axes) for axes in ("yzx", "zyx", "yzx")] + [landing_shapes(8, 384, axes) for axes in ("xz", "zx")]
     scratch += [V((32, 512), BF), V((8, 2048), BF), V((8, n_c), BF), V((2, 4, 8, n_q), BF)]
-    n = 112
+    n = 160
     scratch += [pltpu.SemaphoreType.DMA((n,)), pltpu.SemaphoreType.DMA((n,)), pltpu.SemaphoreType.DMA((32,))]
     s = jax.ShapeDtypeStruct
-    outs = [s((2, 32, 512), F32), s((2, 8, 2048), F32), s((2, 8, n_c), F32), s((2, 4, 8, n_q), F32), s((256, 1024), F32), s((128, 256), F32)]
+    outs = [s((2, 32, 512), BF), s((2, 8, 2048), BF), s((2, 8, n_c), BF), s((2, 4, 8, n_q), BF), s((256, 1024), F32), s((128, 256), F32)]
     anywhere, vm = pl.BlockSpec(memory_space=pl.ANY), pl.BlockSpec(memory_space=pltpu.VMEM)
     return pl.pallas_call(
         reduce_kernel, out_shape=outs, in_specs=[anywhere] * 12 + [vm] * 8, out_specs=[vm] * 6,
@@ -706,13 +715,38 @@
     )(u, dy, n3, dh, att, r1, n2, dcq, catt, r2, datt, dckv, vec_sums, x_all, qkv, lse, wq, e, dx1, vec)
 
 
+def finish_kernel(a, b, c, q, d_qkv, d_self_out, d_cross_q, d_cross_kv, d_cross_out, d_in, d_out, d_gains, d_shifts, d_biases, d_in_bias):
+    for k in range(2):
+        d_out[:, k * 512:(k + 1) * 512] = a[k].astype(F32)
+        d_in[:, k * 2048:(k + 1) * 2048] = b[k].astype(F32)
+        for m, ref in enumerate((d_self_out, d_cross_q, d_cross_out)):
+            ref[:, k * 512:(k + 1) * 512] = c[k, :, m * 512:(m + 1) * 512].astype(F32)
+    for y in range(4):
+        for m in range(3):
+            d_qkv[:, m * 1024 + y * 256:m * 1024 + (y + 1) * 256] = q[0, y, :, m * 256:(m + 1) * 256].astype(F32)
+        for m in range(2):
+            d_cross_kv[:, m * 1024 + y * 256:m * 1024 + (y + 1) * 256] = q[1, y, :, m * 256:(m + 1) * 256].astype(F32)
+    vectors = sum(q[1, y, :, 512:640].astype(F32) for y in range(4)).T
+    for m, ref in enumerate((d_gains, d_shifts, d_biases)):
+        ref[...] = vectors[3 * m:3 * m + 3, :]
+    d_in_bias[...] = vectors[9:13, :]
+
+
+def assembled(a, b, c, q):
+    shapes = [(8, 3072), (8, 1024), (8, 1024), (8, 2048), (8, 1024), (8, 4096), (32, 1024), (3, 8), (3, 8), (3, 8), (4, 8)]
+    vm = pl.BlockSpec(memory_space=pltpu.VMEM)
+    return pl.pallas_call(
+        finish_kernel, out_shape=[jax.ShapeDtypeStruct(s, F32) for s in shapes], in_specs=[vm] * 4, out_specs=[vm] * 11, name="assemble",
+    )(a, b, c, q)
+
+
 def local(tokens, captions, cap_lengths, w_qkv, w_self_out, w_cross_q, w_cross_kv, w_cross_out, w_in, w_out,
           norm_gains, norm_shifts, out_biases, in_bias, out_grad):
     vectors = jnp.concatenate([norm_gains.T, norm_shifts.T, out_biases.T, in_bias.reshape(4, 8).T], axis=1)
-    vectors = jnp.pad(vectors, ((0, 0), (0, 256 - 13)))
+    vectors = jnp.pad(vectors, ((0, 0), (0, 128 - 13)))
     c_in = jnp.concatenate([w_self_out, w_cross_q, w_cross_out], axis=1)
     q_in = jnp.concatenate([w_qkv, w_cross_kv], axis=1).reshape(8, 5, 4, 256).transpose(2, 0, 1, 3).reshape(4, 8, 1280)
-    q_in = jnp.concatenate([q_in, jnp.broadcast_to(vectors, (4, 8, 256))], axis=2)
+    q_in = jnp.concatenate([q_in, jnp.broadcast_to(vectors, (4, 8, 128))], axis=2)
     c_g, win_g, wout_g, x_g, wq, qkv, lse, att, ck, cv, e, vec = gathered(c_in, w_in, w_out, q_in, tokens[0], captions[0])
     wc, full_in, full_out = c_g.reshape(1024, -1), win_g.reshape(1024, -1), wout_g.reshape(4096, 1024)
     hidden_bias = vec[9:13].reshape(4, 128, 8).transpose(1, 0, 2).reshape(1, 4096)
@@ -723,15 +757,8 @@
     vec_sums = jnp.concatenate([sums[:9], d_hidden, jnp.zeros((115, 1024), jnp.float32)], axis=0)
     out_a, out_b, out_c, out_q, tokens_grad, captions_grad = reduced(
         u, dy, n3, dh, att, r1, n2, dcq, catt, r2, datt, dckv, vec_sums, x_g.reshape(1024, 1024), qkv, lse, wq, e, dx1, vec)
-    joined = lambda t: jnp.concatenate([t[0], t[1]], axis=1)
-    q_out = out_q.transpose(2, 1, 0, 3).reshape(8, 4, 1536)
-    vec_out = q_out[:, :, 1280:1293].sum(axis=1)
-    q_out = q_out[:, :, :1280].reshape(8, 4, 5, 256).transpose(0, 2, 1, 3).reshape(8, 5120)
-    return (
-        layer_out[None], tokens_grad[None], captions_grad[None],
-        q_out[:, :3072], joined(out_c[..., :512]), joined(out_c[..., 512:1024]), q_out[:, 3072:], joined(out_c[..., 1024:1536]),
-        joined(out_b), joined(out_a), vec_out[:, :3].T, vec_out[:, 3:6].T, vec_out[:, 6:9].T, vec_out[:, 9:13].T.reshape(32),
-    )
+    *grads, d_in_bias = assembled(out_a, out_b, out_c, out_q)
+    return (layer_out[None], tokens_grad[None], captions_grad[None], *grads, d_in_bias.reshape(32))
 
 
 def solution(mesh):

time: 260 us -> 234 us (0.900)
  Pallas kernels: 235 us -> 216 us
  local copies, waits for them, and re-layouts: 13.5 us -> 9.07 us
    pallas_call x1, Pallas kernels: 94.9 us -> 81.7 us  [gathered(): pl.pallas_call(gather_kernel, out_shape=outs, in_specs=[anywhere] * 6, ou...]
    pallas_call x1, Pallas kernels: 102 us -> 94.1 us  [reduced(): pl.pallas_call(reduce_kernel, out_shape=outs, in_specs=[anywhere] * 12 +...]
    squeeze x3 -> x0, local copies, waits for them, and re-layouts: 2.7 us -> none  [local(): joined = lambda t: jnp.concatenate([t[0], t[1]], axis=1)]
where the time goes in v1:
time: 234 us; the launch traced here: 233 us
  Pallas kernels  216 us (92%)
  local copies, waits for them, and re-layouts  9.07 us (4%)
  other arithmetic  6.72 us (3%)
    pallas_call x1, Pallas kernels, reduced(): pl.pallas_call(reduce_kernel, out_shape=outs, in_specs=[anywhere] * 12 +...  94.1 us
    pallas_call x1, Pallas kernels, gathered(): pl.pallas_call(gather_kernel, out_shape=outs, in_specs=[anywhere] * 6, ou...  81.7 us
    pallas_call x1, Pallas kernels, middle(): pl.pallas_call(middle_kernel, out_shape=outs, in_specs=[pl.BlockSpec(memo...  38.2 us

profile of v1, /device:TPU:1, one launch (start us, length us, event | category | flops | bytes accessed | tf_op | source)
XLA Modules:
  0.0 233.0 jit_solution(2382770538175622959)
XLA Ops:
  0.6 0.8 pad_maximum_fusion.1
  1.5 0.7 reshape.66
  2.2 0.7 pad_maximum_fusion.3
  2.9 0.1 copy.37
  3.1 0.6 pad_maximum_fusion.q_in
  3.7 1.4 pad_maximum_fusion.2.c_in
  5.1 81.7 %gather_and_attend.1 = (bf16[4,4,2,4,8,3072]{5,4,3,2,1,0:T(8,128)(2,1)}, bf16[4,4,2,4,8,4096]{5,4,3,2,1,0:T(8,128)(2,1)}, bf16[4,4,2,4,32,1024]{5,4,3,2,1,0:T(8,...) custom-call(bf16[8,3072]{1,0:T(8,128)(2,1)} %pad_maximum_fusion.2.c_, ...), custom_call_target="tpu_custom_call" | custom-call | tf_op jit(solution)/shard_map/gather_and_attend/pallas_call | solution.py:454
  86.8 0.8 slice.6
  87.6 0.2 reshape.67
  87.7 0.2 copy.35
  87.9 0.9 reshape.68.inb
  89.4 38.2 %middle.1 = (bf16[256,1024]{1,0:T(8,128)(2,1)}, f32[256,1024]{1,0:T(8,128)}, bf16[256,1024]{1,0:T(8,128)(2,1)}, bf16[128,2048]{1,0:T(8,128)(2,1)}, bf16[256,1024...) custom-call(s32[1]{0:T(128)S(6)} %copy.40.length, ...), custom_call_target="tpu_custom_call" | custom-call | tf_op jit(solution)/shard_map/middle/pallas_call | solution.py:270
  127.6 0.5 broadcast.7
  128.1 1.4 reduce.3
  129.5 0.3 reshape.72
  129.9 0.2 reshape.73
  130.1 0.1 pad.7.clone
  130.2 1.7 maximum_maximum_fusion.vec_sums
  131.9 94.1 %reduce_gradients.1 = (bf16[2,32,512]{2,1,0:T(8,128)(2,1)}, bf16[2,8,2048]{2,1,0:T(8,128)(2,1)}, bf16[2,8,1536]{2,1,0:T(8,128)(2,1)}, bf16[2,4,8,768]{3,2,1,0:T(...) custom-call(bf16[256,4096]{1,0:T(8,128)(2,1)} %get-tuple-element.65.u, bf16[256,1024]{1,0:T(8,128)(2,1)} %bitcast.26, ...), custom_call_target="tpu_custom_call" | custom-call | tf_op jit(solution)/shard_map/reduce_gradients/pallas_call | solution.py:710
  226.1 1.8 assemble.1
  227.8 1.3 reshape.75
  229.1 2.3 copy.41
  231.4 1.6 copy.42
  (5 shorter events, 0.0 us)

commit v2 on v1

v2 whole, which is shorter than its diff:
```python
import functools

import jax
import jax.numpy as jnp
from jax import lax
from jax.experimental import pallas as pl
from jax.experimental.pallas import tpu as pltpu
from jax.sharding import PartitionSpec as P

MESH = pl.DeviceIdType.MESH
def position():
    dp, y = lax.axis_index("dp"), lax.axis_index("seq")
    return {"z": lax.div(dp, 8), "x": lax.rem(lax.div(dp, 2), 4), "c": lax.rem(dp, 2), "y": y}


def device(at):
    return (at["z"] * 8 + at["x"] * 2 + at["c"], at["y"])


def moved(at, axis, by):
    size = 2 if axis == "c" else 4
    return {**at, axis: lax.rem(at[axis] + by + size, size)}


class Copies:
    def __init__(self, send, recv):
        self.send, self.recv, self.used = send, recv, 0

    def start(self, src, dst, at):
        k = self.used
        self.used += 1
        assert k < self.send.shape[0]
        copy = pltpu.make_async_remote_copy(src_ref=src, dst_ref=dst, send_sem=self.send.at[k], recv_sem=self.recv.at[k], device_id=device(at), device_id_type=MESH)
        copy.start()
        return copy


def block(ref, at, whole, cols):
    idx = [slice(None) if axis in whole else at[axis] for axis in ("z", "x", "c", "y")]
    return ref.at[(*idx, slice(None), cols)]


def gather_flow(ref, at, cols, axes, whole, copies, partner, done, source=None):
    start, size = cols
    low_cols, high_cols = pl.ds(start, size // 256 * 128), pl.ds(start + size // 256 * 128, size - size // 256 * 128)
    cols = pl.ds(start, size)
    whole = set(whole)
    for axis in axes:
        up, down = moved(at, axis, 1), moved(at, axis, -1)
        own = block(ref, at, whole, cols)
        src = own if source is None else source.at[:, cols]
        source = None
        a = copies.start(src, own, up)
        b = copies.start(src, own, down)
        yield
        a.wait_recv()
        b.wait_recv()
        low, high = block(ref, down, whole, low_cols), block(ref, up, whole, high_cols)
        c = copies.start(low, low, up)
        d = copies.start(high, high, down)
        for p in (down, up):
            got = block(ref, p, whole, cols)
            done.append(copies.start(got, got, partner))
        yield
        c.wait_recv()
        d.wait_recv()
        far = block(ref, moved(at, axis, 2), whole, cols)
        done.append(copies.start(far, far, partner))
        for s in (a, b, c, d):
            s.wait_send()
        whole.add(axis)


EPSILON = 1e-05
MASKED = -1e30
SCALE = 64 ** -0.5
BF, F32 = jnp.bfloat16, jnp.float32
def mm(a, b):
    return jnp.dot(a, b, preferred_element_type=F32)


def mm_rows(a, b):
    return lax.dot_general(a, b, (((0,), (0,)), ((), ())), preferred_element_type=F32)


def mm_cols(a, b):
    return lax.dot_general(a, b, (((1,), (1,)), ((), ())), preferred_element_type=F32)


def normed(v):
    centred = v - jnp.mean(v, axis=-1, keepdims=True)
    r = lax.rsqrt(jnp.mean(centred * centred, axis=-1, keepdims=True) + EPSILON)
    return centred * r, r


def norm_back(v, d, gain):
    z, r = normed(v)
    w = d * gain
    dv = r * (w - jnp.mean(w, axis=-1, keepdims=True) - z * jnp.mean(w * z, axis=-1, keepdims=True))
    return dv, jnp.sum(d * z, axis=0, keepdims=True), jnp.sum(d, axis=0, keepdims=True)


def loop(n, body):
    def step(i, _):
        body(i)
        return 0

    lax.fori_loop(0, n, step, 0)


def gelu_both(h):
    cdf = 0.5 * (1.0 + lax.erf(h * (0.5 ** 0.5)))
    return h * cdf, cdf + h * jnp.exp(-0.5 * h * h) * (1.0 / (2.0 * 3.141592653589793) ** 0.5)


def lanes_of(pair_shape, head):
    lane = lax.broadcasted_iota(jnp.int32, pair_shape, 1)
    return (lane < 64) if head == 0 else (lane >= 64)


BLOCK = 256
def causal_keep(n, at):
    keys = lax.broadcasted_iota(jnp.int32, (n, BLOCK), 0)
    return keys <= lax.broadcasted_iota(jnp.int32, (n, BLOCK), 1) + at


def project(x, wq, vec, n1, qkv):
    def rows(i):
        r = pl.ds(pl.multiple_of(i * 128, 128), 128)
        z, _ = normed(x[r, :].astype(F32))
        n1[r, :] = (z * vec[0:1, :] + vec[3:4, :]).astype(BF)

    loop(8, rows)

    def cols(i):
        r = pl.ds(pl.multiple_of(i * BLOCK, BLOCK), BLOCK)
        qkv[r, :] = mm(n1[r, :], wq[:, 0:768]).astype(BF)

    loop(4, cols)


def self_forward(qkv, att, lse):
    def pair(p):
        for i in range(1024 // BLOCK):
            n, r = (i + 1) * BLOCK, slice(i * BLOCK, (i + 1) * BLOCK)
            at = lambda part: pl.ds(pl.multiple_of(part * 256 + p * 128, 128), 128)
            q, k, v = qkv[r, at(0)], qkv[0:n, at(1)], qkv[0:n, at(2)]
            keep = causal_keep(n, i * BLOCK)
            mixed = []
            for head in range(2):
                qh = jnp.where(lanes_of(q.shape, head), q, jnp.zeros_like(q))
                s = jnp.where(keep, mm_cols(k, qh) * SCALE, MASKED)
                top = jnp.max(s, axis=0, keepdims=True)
                e = jnp.exp(s - top)
                total = jnp.sum(e, axis=0, keepdims=True)
                lse[2 * p + head, :, r] = top + jnp.log(total)
                mixed.append(mm_rows((e * (1.0 / total)).astype(BF), v))
            att[r, at(0)] = jnp.where(lanes_of(q.shape, 0), mixed[0], mixed[1]).astype(BF)

    loop(2, pair)


def self_backward(p, qkv, lse, datt, dqkv, dk, dv):
    def pair(p):
        at = lambda part: pl.ds(part * 256 + p * 128, 128)
        dk[...] = jnp.zeros_like(dk)
        dv[...] = jnp.zeros_like(dv)
        for i in range(1024 // BLOCK):
            n, r = (i + 1) * BLOCK, slice(i * BLOCK, (i + 1) * BLOCK)
            q, k, v, d = qkv[r, at(0)], qkv[0:n, at(1)], qkv[0:n, at(2)], datt[r, at(0)]
            keep = causal_keep(n, i * BLOCK)
            dq = []
            for head in range(2):
                lanes = lanes_of(q.shape, head)
                qh = jnp.where(lanes, q, jnp.zeros_like(q))
                dout = jnp.where(lanes, d, jnp.zeros_like(d))
                prob = jnp.where(keep, jnp.exp(mm_cols(k, qh) * SCALE - lse[2 * p + head, :, r]), 0.0)
                dp = mm_cols(v, dout)
                ds = (prob * (dp - jnp.sum(dp * prob, axis=0, keepdims=True))).astype(BF)
                dv[0:n, :] += mm(prob.astype(BF), dout)
                dk[0:n, :] += mm(ds, qh)
                dq.append(mm_rows(ds, k))
            dqkv[r, at(0)] = (jnp.where(lanes_of(q.shape, 0), dq[0], dq[1]) * SCALE).astype(BF)
        dqkv[:, at(1)] = (dk[...] * SCALE).astype(BF)
        dqkv[:, at(2)] = dv[...].astype(BF)

    pair(p)


def greet(others):
    barrier = pltpu.get_barrier_semaphore()
    for o in others:
        pl.semaphore_signal(barrier, inc=1, device_id=device(o), device_id_type=MESH)
    pl.semaphore_wait(barrier, len(others))


def half(n, of):
    return pl.ds(pl.multiple_of(of["c"] * (n // 2), 128), n // 2)


def finish(flows):
    live = list(flows)
    while live:
        for f in list(live):
            if next(f, "end") == "end":
                live.remove(f)


def quarter(of):
    return pl.ds(pl.multiple_of(of["y"] * 256, 256), 256)


def cross_forward(p, length, ck, cv, cq, probs, catt):
    cols = pl.ds(pl.multiple_of(p * 128, 128), 128)
    k, v, q = ck[:, cols], cv[:, cols], cq[:, cols]
    seen = lax.broadcasted_iota(jnp.int32, (128, 256), 0) < length
    mixed = []
    for head in range(2):
        qh = jnp.where(lanes_of(q.shape, head), q, jnp.zeros_like(q))
        s = jnp.where(seen, mm_cols(k, qh) * SCALE, MASKED)
        e = jnp.exp(s - jnp.max(s, axis=0, keepdims=True))
        prob = e / jnp.sum(e, axis=0, keepdims=True)
        probs[2 * p + head] = prob
        mixed.append(mm_rows(prob.astype(BF), v))
    catt[:, cols] = jnp.where(lanes_of(q.shape, 0), mixed[0], mixed[1]).astype(BF)


def gather_kernel(length, w_qkv, w_ckv, w_so, w_cq, w_co, vectors, win_in, wout_in, x_in, cap_in, dy_in,
                  c_out, win_g, wout_g, dy_o, x_out, wq_out, qkv_out, lse_out, att_out, ck_out, cv_out, e_out, x1_out, x2_out, n2_out, n3_out,
                  catt_out, probs_out, cq_out, vec, wide_o,
                  x_g, wq_o, qkv, lse, att_o, ck_o, cv_o, e_o, x1, x2, n2_o, n3_o, catt_o, probs, cq,
                  q_in, c_in, c_g, q_g, n1, att, ckv, send, recv, local):
    at = position()
    partner = moved(at, "c", 1)
    row = [moved(at, "y", b) for b in (1, 3, 2)]
    q_in[:, :, 1280:1408] = jnp.broadcast_to(vectors[...], (4, 8, 128))
    for q in range(4):
        for m in range(3):
            q_in[q, :, m * 256:(m + 1) * 256] = w_qkv[:, m * 1024 + q * 256:m * 1024 + (q + 1) * 256]
        for m in range(2):
            q_in[q, :, 768 + m * 256:1024 + m * 256] = w_ckv[:, m * 1024 + q * 256:m * 1024 + (q + 1) * 256]
    for m, ref in enumerate((w_so, w_cq, w_co)):
        c_in[:, m * 1024:(m + 1) * 1024] = ref[...]
    greet([moved(at, a, b) for a in "zx" for b in (1, -1)] + row + [partner])
    copies = Copies(send, recv)
    me = (at["z"], at["x"], at["c"], at["y"])
    kept, sent = [], []

    def keep(src, dst):
        cp = pltpu.make_async_copy(src, dst, local.at[len(kept)])
        cp.start()
        kept.append(cp)
        return cp

    keep(q_in.at[at["y"]], q_g.at[me])
    qx = [copies.start(q_in.at[to["y"]], q_g.at[me], to) for to in row]
    q_done, c_done, done = [], [], []
    fc = [gather_flow(c_g, at, (0, 1536), "xzy", (), copies, partner, c_done, c_in),
          gather_flow(c_g, at, (1536, 1536), "zxy", (), copies, partner, c_done, c_in)]
    fab = [gather_flow(dst, at, (k * n, n), axes, (), copies, partner, done, src)
           for k in range(2) for src, dst, axes, n in ((wout_in, wout_g, "yzx", 512), (win_in, win_g, "yxz", 2048))]
    flows = fab[0:2] + fc[0:1] + fab[2:4] + fc[1:2]
    for f in flows:
        next(f)
    keep(x_in, x_g.at[at["y"]])
    up, down = row[0], row[1]
    keep(cap_in, e_o.at[:, quarter(at)])
    ee = [copies.start(cap_in, e_o.at[:, quarter(at)], to) for to in row]
    for src, dst, to in ((wout_in, wout_g, done), (win_in, win_g, done), (c_in, c_g, c_done)):
        keep(src, dst.at[me])
        to.append(copies.start(src, dst.at[me], partner))
    for s in [kept[0]] + qx:
        s.wait()
    q_own = block(q_g, at, {"y"}, slice(None))
    q_done.append(copies.start(q_own, q_own, partner))
    fq = [gather_flow(q_g, at, (0, 640), "zx", {"y"}, copies, partner, q_done),
          gather_flow(q_g, at, (640, 768), "xz", {"y"}, copies, partner, q_done)]
    for f in fq:
        next(f)
    for s in kept[1:]:
        s.wait()
    for k in range(4):
        for f in fq:
            next(f, None)
        for f in flows:
            next(f)
        if k == 0:
            xx = [copies.start(x_in, x_g.at[at["y"]], to) for to in (up, down)]
        if k == 1:
            for s in xx:
                s.wait()
            low, high = slice(0, 128), slice(128, 256)
            x2s = [copies.start(x_g.at[down["y"], low], x_g.at[down["y"], low], up),
                   copies.start(x_g.at[up["y"], high], x_g.at[up["y"], high], down)]
    for s in x2s + ee + q_done:
        s.wait()

    wide = q_g[:, :, :, :, :, 1280:1408].reshape(1024, 128)
    wide_o[...] = wide
    vec[...] = wide.astype(F32).T[0:16, :]
    wq_o[...] = q_g[:, :, :, :, :, 0:1280].reshape(1024, 1280)
    done.append(keep(x_g, x_out))
    done.append(keep(wq_o, wq_out))
    done.append(keep(e_o, e_out))
    project(x_g.reshape(1024, 1024), wq_o, vec, n1, qkv)
    done.append(keep(qkv, qkv_out))
    ckv[...] = mm(e_o[...], wq_o[:, 768:1280]).astype(BF)
    self_forward(qkv, att, lse)
    done.append(keep(lse, lse_out))
    own, theirs = pl.ds(0, 256), pl.ds(256, 256)
    for to in row:
        sent.append(copies.start(att.at[quarter(to)], att_o.at[:, quarter(at)], to))
        sent.append(copies.start(ckv.at[:, 0:256], ck_o.at[:, quarter(at)], to))
        sent.append(copies.start(ckv.at[:, 256:512], cv_o.at[:, quarter(at)], to))
    sent.append(keep(att.at[quarter(at)], att_o.at[:, quarter(at)]))
    sent.append(keep(ckv.at[:, 0:256], ck_o.at[:, quarter(at)]))
    sent.append(keep(ckv.at[:, 256:512], cv_o.at[:, quarter(at)]))
    done.append(keep(dy_in.at[:, half(1024, at)], dy_o.at[own]))
    done.append(copies.start(dy_in.at[:, half(1024, partner)], dy_o.at[theirs], partner))
    for f in fc:
        next(f)
    for f in fc:
        next(f, None)
    for f in fab:
        next(f)
    for s in sent + c_done:
        s.wait()

    done.append(keep(c_g, c_out))
    done.append(keep(ck_o, ck_out))
    done.append(keep(cv_o, cv_out))

    def hand_over(ref, to):
        done.append(copies.start(ref, to.at[theirs], partner))
        done.append(keep(ref, to.at[own]))

    def square(m):
        return c_g[:, :, :, :, :, m * 1024:(m + 1) * 1024].reshape(1024, 1024)

    hand_over(att_o, att_out)
    x1[...] = mm(att_o[...], square(0))

    def by_rows(body):
        loop(4, lambda i: body(pl.ds(pl.multiple_of(i * 64, 64), 64)))

    def after_self(r):
        v = x_g[at["y"], r, :].astype(F32) + x1[r, :] + vec[6:7, :]
        x1[r, :] = v
        z, _ = normed(v)
        n2_o[r, :] = (z * vec[1:2, :] + vec[4:5, :]).astype(BF)

    by_rows(after_self)
    done.append(keep(x1, x1_out))
    hand_over(n2_o, n2_out)
    cq[...] = mm(n2_o[...], square(1)).astype(BF)
    done.append(keep(cq, cq_out))
    loop(8, lambda p: cross_forward(p, length[0], ck_o, cv_o, cq, probs, catt_o))
    done.append(keep(probs, probs_out))
    hand_over(catt_o, catt_out)
    x2[...] = mm(catt_o[...], square(2))

    def after_cross(r):
        v = x1[r, :] + x2[r, :] + vec[7:8, :]
        x2[r, :] = v
        z, _ = normed(v)
        n3_o[r, :] = (z * vec[2:3, :] + vec[5:6, :]).astype(BF)

    by_rows(after_cross)
    done.append(keep(x2, x2_out))
    hand_over(n3_o, n3_out)
    for f in fab:
        next(f, None)
    for s in done:
        s.wait()


def gathered(length, w_qkv, w_ckv, w_so, w_cq, w_co, vectors, win_in, wout_in, x_in, cap_in, dy_in):
    s = jax.ShapeDtypeStruct
    anywhere, vm = pl.BlockSpec(memory_space=pl.ANY), pl.BlockSpec(memory_space=pltpu.VMEM)
    kept = [((4, 256, 1024), BF), ((1024, 1280), BF), ((1024, 768), BF), ((4, 1, 1024), F32), ((512, 1024), BF), ((128, 1024), BF),
            ((128, 1024), BF), ((128, 1024), BF), ((256, 1024), F32), ((256, 1024), F32), ((512, 1024), BF), ((512, 1024), BF),
            ((512, 1024), BF), ((16, 128, 256), F32), ((256, 1024), BF)]
    outs = [s((4, 4, 2, 4, 8, 3072), BF), s((4, 4, 2, 4, 8, 4096), BF), s((4, 4, 2, 4, 32, 1024), BF), s((512, 512), BF)]
    outs += [s(*o) for o in kept] + [s((16, 1024), F32), s((1024, 128), BF)]
    n = 196
    mine = [pltpu.VMEM((256, 1024) if shape == (512, 1024) else shape, kind) for shape, kind in kept]
    return pl.pallas_call(
        gather_kernel, out_shape=outs, in_specs=[pl.BlockSpec(memory_space=pltpu.SMEM)] + [vm] * 6 + [anywhere] * 5,
        out_specs=[anywhere] * 19 + [vm] * 2,
        scratch_shapes=mine + [pltpu.VMEM((4, 8, 1408), BF), pltpu.VMEM((8, 3072), BF), pltpu.VMEM((4, 4, 2, 4, 8, 3072), BF),
                        pltpu.VMEM((4, 4, 2, 4, 8, 1408), BF), pltpu.VMEM((1024, 1024), BF), pltpu.VMEM((1024, 256), BF), pltpu.VMEM((128, 512), BF),
                        pltpu.SemaphoreType.DMA((n,)), pltpu.SemaphoreType.DMA((n,)), pltpu.SemaphoreType.DMA((40,))],
        compiler_params=pltpu.CompilerParams(collective_id=0, has_side_effects=True, vmem_limit_bytes=60 << 20),
        name="gather_and_attend",
    )(length, w_qkv, w_ckv, w_so, w_cq, w_co, vectors, win_in, wout_in, x_in, cap_in, dy_in)


def middle_kernel(x2_in, n3_in, dy_in, vec, wide, x1_in, probs_in, cq_in, ck_in, cv_in, wc, win, wout,
                  out, dx1_o, datt_o, dckv_o, u_o, dh_o, r1_o, dcq_o, r2_o, sums,
                  so, wcq, co, wi, wo, x1, x2, probs, cq, ck, cv, ya, dn, dca, dh, r1, dcq, r2, n3, spread, sem, send, recv):
    at = position()
    partner = moved(at, "c", 1)
    barrier = pltpu.get_barrier_semaphore()
    pl.semaphore_signal(barrier, inc=1, device_id=device(partner), device_id_type=MESH)
    chunk = 512
    n_chunk = wi.shape[1] // chunk
    width = 8 * chunk // 32

    def ff_loads(i):
        cols = pl.ds(pl.multiple_of(i * chunk, chunk), chunk)
        return (pltpu.make_async_copy(win.at[:, cols], wi.at[:, cols], sem.at[2 * i]),
                pltpu.make_async_copy(wout.at[cols], wo.at[cols], sem.at[2 * i + 1]))

    n3_load = pltpu.make_async_copy(n3_in.at[pl.ds(0, 256)], n3, sem.at[39])
    n3_load.start()
    for i in range(n_chunk):
        for l in ff_loads(i):
            l.start()
    late = [(wc.at[:, pl.ds(2048, 1024)], co), (probs_in, probs), (cq_in, cq), (ck_in, ck), (cv_in, cv),
            (wc.at[:, pl.ds(1024, 1024)], wcq), (x1_in, x1), (wc.at[:, pl.ds(0, 1024)], so)]
    late = [pltpu.make_async_copy(a, b, sem.at[2 * n_chunk + k]) for k, (a, b) in enumerate(late)]
    for l in late:
        l.start()

    def by_rows(body):
        loop(4, lambda i: body(pl.ds(pl.multiple_of(i * 64, 64), 64)))

    def row(k):
        return vec[k:k + 1, :]

    def place(shape, at_row, at_unit):
        src, dst = lax.broadcasted_iota(jnp.int32, shape, at_row), lax.broadcasted_iota(jnp.int32, shape, at_unit)
        return (lax.div(src, 8) * 32 + lax.rem(src, 8)), dst

    for j in range(4):
        src, dst = place((width, chunk), 0, 1)
        spread[j] = jnp.where(src + 8 * j == dst, 1.0, 0.0).astype(BF)

    sums[...] = jnp.zeros_like(sums)
    ya[...] = jnp.zeros_like(ya)
    dn[...] = jnp.zeros_like(dn)

    def feed(i):
        for l in ff_loads(i):
            l.wait()
        cols = pl.ds(pl.multiple_of(i * chunk, chunk), chunk)
        part = pl.ds(pl.multiple_of(i * width, width), width)
        columns = wide[part, :].astype(F32).T.astype(BF)
        bias = sum(mm(columns[9 + j:10 + j, :], spread[j]) for j in range(4))
        h = mm(n3[...], wi[:, cols]) + bias
        u, slope = gelu_both(h)
        u = u.astype(BF)
        u_o[0:256, cols] = u
        ya[...] += mm(u, wo[cols, :])
        d = (mm_cols(dy_in[...], wo[cols, :]) * slope).astype(BF)
        dh[:, cols] = d
        total = jnp.sum(d.astype(F32), axis=0, keepdims=True)
        high = total.astype(BF)
        low = (total - high.astype(F32)).astype(BF)
        for j in range(4):
            sums[9 + j:10 + j, part] = mm_cols(high, spread[j]) + mm_cols(low, spread[j])
        dn[...] += mm_cols(d, wi[:, cols])

    n3_load.wait()
    loop(n_chunk, feed)
    pl.semaphore_wait(barrier, 1)
    copies = Copies(send, recv)
    own, theirs = pl.ds(0, 256), pl.ds(256, 256)
    sent = [copies.start(u_o.at[own], u_o.at[theirs], partner)]

    def share(src, dst):
        n = src.shape[1]
        cp = pltpu.make_async_copy(src.at[:, half(n, at)], dst.at[own], sem.at[2 * n_chunk + 8 + len(sent)])
        cp.start()
        sent.append(cp)
        sent.append(copies.start(src.at[:, half(n, partner)], dst.at[theirs], partner))

    share(dh, dh_o)

    def after_feed(r):
        v = x2_in[r, :]
        out[r, :] = (v + ya[r, :] + row(8)).astype(BF)
        dy = dy_in[r, :].astype(F32)
        dv, dgain, dshift = norm_back(v, dn[r, :], row(2))
        d = dy + dv
        x2[r, :] = d
        r2[r, :] = d.astype(BF)
        sums[2:3, :] += dgain
        sums[5:6, :] += dshift
        sums[7:8, :] += jnp.sum(d, axis=0, keepdims=True)
        sums[8:9, :] += jnp.sum(dy, axis=0, keepdims=True)

    by_rows(after_feed)
    share(r2, r2_o)

    for l in late[:5]:
        l.wait()
    dca[...] = mm_cols(r2[...], co[...]).astype(BF)

    def cross_backward(p):
        cols = pl.ds(pl.multiple_of(p * 128, 128), 128)
        k, v, q, d = ck[:, cols], cv[:, cols], cq[:, cols], dca[:, cols]
        dk = dv = jnp.zeros((128, 128), F32)
        dq = []
        for head in range(2):
            lanes = lanes_of(q.shape, head)
            qh = jnp.where(lanes, q, jnp.zeros_like(q))
            dout = jnp.where(lanes, d, jnp.zeros_like(d))
            prob = probs[2 * p + head]
            dp = mm_cols(v, dout)
            ds = (prob * (dp - jnp.sum(dp * prob, axis=0, keepdims=True))).astype(BF)
            dv += mm(prob.astype(BF), dout)
            dk += mm(ds, qh)
            dq.append(mm_rows(ds, k))
        dcq[:, cols] = (jnp.where(lanes_of(q.shape, 0), dq[0], dq[1]) * SCALE).astype(BF)
        dckv_o[:, cols] = (dk * SCALE).astype(BF)
        dckv_o[:, pl.ds(pl.multiple_of(1024 + p * 128, 128), 128)] = dv.astype(BF)

    loop(8, cross_backward)
    share(dcq, dcq_o)
    for l in late[5:]:
        l.wait()
    dn[...] = mm_cols(dcq[...], wcq[...])

    def before_cross(r):
        dv, dgain, dshift = norm_back(x1[r, :], dn[r, :], row(1))
        d = x2[r, :] + dv
        dx1_o[r, :] = d
        r1[r, :] = d.astype(BF)
        sums[1:2, :] += dgain
        sums[4:5, :] += dshift
        sums[6:7, :] += jnp.sum(d, axis=0, keepdims=True)

    by_rows(before_cross)
    share(r1, r1_o)
    datt_o[...] = mm_cols(r1[...], so[...]).astype(BF)
    for s in sent:
        s.wait()


def middle(x2, n3, dy, vec, wide, x1, probs, cq, ck, cv, wc, win, wout):
    s, V = jax.ShapeDtypeStruct, pltpu.VMEM
    outs = [s((256, 1024), BF), s((256, 1024), F32), s((256, 1024), BF), s((128, 2048), BF), s((512, 4096), BF), s((512, 2048), BF),
            s((512, 512), BF), s((512, 512), BF), s((512, 512), BF), s((16, 1024), F32)]
    vm, anywhere = pl.BlockSpec(memory_space=V), pl.BlockSpec(memory_space=pl.ANY)
    scratch = [V((1024, 1024), BF)] * 3 + [V((1024, 4096), BF), V((4096, 1024), BF)]
    scratch += [V((256, 1024), F32)] * 2 + [V((16, 128, 256), F32), V((256, 1024), BF), V((128, 1024), BF), V((128, 1024), BF)]
    scratch += [V((256, 1024), F32)] * 2 + [V((256, 1024), BF), V((256, 4096), BF)] + [V((256, 1024), BF)] * 4 + [V((4, 128, 512), BF)]
    scratch += [pltpu.SemaphoreType.DMA((40,)), pltpu.SemaphoreType.DMA((8,)), pltpu.SemaphoreType.DMA((8,))]
    return pl.pallas_call(
        middle_kernel, out_shape=outs,
        in_specs=[vm, anywhere] + [vm] * 3 + [anywhere] * 8, out_specs=[vm] * 4 + [vm] * 1 + [anywhere] * 4 + [vm],
        scratch_shapes=scratch,
        compiler_params=pltpu.CompilerParams(collective_id=2, has_side_effects=True, vmem_limit_bytes=60 << 20),
        name="middle",
    )(x2, n3, dy, vec, wide, x1, probs, cq, ck, cv, wc, win, wout)


ORDER = ("z", "x", "c", "y")
def part(ref, at, whole, **fixed):
    return ref.at[tuple(fixed[a] if a in fixed else slice(None) if a in whole else at[a] for a in ORDER)]


def each(shape, body):
    total = 1
    for s in shape:
        total *= s

    def step(i, _):
        index, rest = [], i
        for s in reversed(shape):
            index.insert(0, lax.rem(rest, s))
            rest = lax.div(rest, s)
        body(tuple(index))
        return 0

    if total == 1:
        body((0,) * len(shape))
    else:
        lax.fori_loop(0, total, step, 0)


def add_into(dst, *srcs):
    def one(index):
        total = dst[index].astype(jnp.float32)
        for s in srcs:
            total += s[index].astype(jnp.float32)
        dst[index] = total.astype(dst.dtype)

    each(dst.shape[:-2], one)


def landing_shapes(rows, cols, axes):
    whole, shapes = {"z", "x", "y"}, []
    for axis in axes:
        whole = whole - {axis}
        shapes.append(pltpu.VMEM((6, *[4 for a in ("z", "x", "y") if a in whole], rows, cols), jnp.bfloat16))
    return tuple(shapes)


def scatter_flow(g, landing, at, axes, whole, copies):
    whole = set(whole)
    for axis, land in zip(axes, landing):
        up, down, far = moved(at, axis, 1), moved(at, axis, -1), moved(at, axis, 2)
        rest = whole - {axis}
        def blk(place, core):
            return part(g, at, rest, **{axis: place[axis], "c": core})
        s = [
            copies.start(blk(far, 0), land.at[0], up),
            copies.start(blk(far, 1), land.at[1], down),
        ]
        if axis == axes[0]:
            yield
        s += [copies.start(blk(up, 1), land.at[2], up), copies.start(blk(down, 0), land.at[3], down)]
        yield
        s[0].wait_recv()
        add_into(blk(up, 0), land.at[0])
        s.append(copies.start(blk(up, 0), land.at[4], up))
        s[1].wait_recv()
        add_into(blk(down, 1), land.at[1])
        s.append(copies.start(blk(down, 1), land.at[5], down))
        yield
        s[2].wait_recv()
        s[5].wait_recv()
        add_into(blk(at, 1), land.at[2], land.at[5])
        s[3].wait_recv()
        s[4].wait_recv()
        add_into(blk(at, 0), land.at[3], land.at[4])
        for q in s:
            q.wait_send()
        whole = rest


def reduce_kernel(u, dy, n3, dh, att, r1, n2, dcq, catt, r2, datt, dckv, sums, x_in, qkv_in, lse, wq_in, e, dx1_in, vec,
                  out_a, out_b, out_c, out_q, tok, cap,
                  u2, dy2, n32, dh2, a2, r2s, ga, gb, gc, gq, gql, datt4, dckv4, dcap, dcap4, dqkv, n1, dk, dv, dn, dn4, v13, x_all, qkv, wq, dx1,
                  la, lb, lc0, lc1, lc2, lq0, lq1, fa, fb, fc, fq, send, recv, local):
    at = position()
    partner = moved(at, "c", 1)
    row = [moved(at, "y", b) for b in (1, 3, 2)]
    ring = row + [moved(o, "c", 1) for o in row] + [partner]
    c, y = at["c"], at["y"]
    started = []

    def load(src, dst):
        cp = pltpu.make_async_copy(src, dst, local.at[len(started)])
        cp.start()
        started.append(cp)
        return cp

    def ready(loads):
        for l in loads:
            l.wait()

    kb = [load(n3, n32), load(dh, dh2)]
    ka = [load(u, u2), load(dy, dy2)]
    own_rows = pl.ds(pl.multiple_of(y * 256, 256), 256)
    d_own = load(datt.at[:, quarter(at)], datt4.at[own_rows])
    kv_own = [load(dckv.at[:, pl.ds(pl.multiple_of(k * 1024 + y * 256, 256), 256)], dckv4.at[y, :, pl.ds(k * 256, 256)]) for k in range(2)]
    kp = [load(qkv_in, qkv), load(wq_in, wq), load(x_in, x_all)]
    kc = []
    for k, (a, b) in enumerate(((catt, r2), (n2, dcq), (att, r1))):
        kc += [load(a, a2.at[k]), load(b, r2s.at[k])]
    kp.append(load(dx1_in, dx1))
    greet([moved(at, a, b) for a in "zx" for b in (1, -1)] + ring)
    copies = Copies(send, recv)
    dd = [copies.start(datt.at[:, quarter(to)], datt4.at[own_rows], to) for to in row]
    kvs = [copies.start(dckv.at[:, pl.ds(pl.multiple_of(k * 1024 + to["y"] * 256, 256), 256)], dckv4.at[y, :, pl.ds(k * 256, 256)], to)
           for to in row for k in range(2)]

    def grad_b(z):
        lhs = n32[:, pl.ds(pl.multiple_of(z * 256, 256), 256)]
        for k in range(4):
            g = mm_rows(lhs, dh2[:, k * 512:(k + 1) * 512])
            gb[z, :, :, :, :, k * 512:(k + 1) * 512] = g.reshape(4, 2, 4, 8, 512).astype(BF)

    def grad_a(z, x):
        lhs = u2[:, pl.ds(pl.multiple_of((z * 4 + x) * 256, 256), 256)]
        ga[z, x] = mm_rows(lhs, dy2[...]).reshape(2, 4, 32, 512).astype(BF)

    def grad_c(k, z):
        g = mm_rows(a2[k, :, pl.ds(pl.multiple_of(z * 256, 256), 256)], r2s[k])
        gc[z, :, :, :, :, k * 512:(k + 1) * 512] = g.reshape(4, 2, 4, 8, 512).astype(BF)

    every = {"z", "x", "y"}
    fl_b = scatter_flow(gb, lb, at, ("z", "x", "y"), every, copies)
    fl_a = scatter_flow(ga, la, at, ("x", "z", "y"), every, copies)
    fl_c = [scatter_flow(gc.at[:, :, :, :, :, pl.ds(k * 512, 512)], land, at, axes, every, copies)
            for k, (land, axes) in enumerate(((lc0, "zxy"), (lc1, "xzy"), (lc2, "yzx")))]
    far_z, far_x = moved(at, "z", 2)["z"], moved(at, "x", 2)["x"]
    ready(kb)
    grad_b(far_z)
    next(fl_b)
    ready(ka)
    loop(4, lambda i: grad_a(i, far_x))
    next(fl_a)
    loop(3, lambda i: grad_b(lax.rem(far_z + 1 + i, 4)))
    next(fl_b)
    loop(12, lambda i: grad_a(lax.rem(i, 4), lax.rem(far_x + 1 + lax.div(i, 4), 4)))
    next(fl_a)
    ready(kc)
    for k in range(3):
        loop(4, functools.partial(grad_c, k))
        next(fl_c[k])
        next(fl_c[k])

    ready(kp)
    for s in kv_own + kvs:
        s.wait()
    dckv4[0] = sum(dckv4[k].astype(F32) for k in range(4)).astype(BF)
    dcap[...] = mm_cols(dckv4[0], wq[:, 768:1280]).astype(BF)
    cap_own = load(dcap.at[:, quarter(at)], dcap4.at[y])
    caps = [copies.start(dcap.at[:, quarter(to)], dcap4.at[y], to) for to in row]

    d_own.wait()
    for s in dd:
        s.wait()
    self_backward(0, qkv, lse, datt4, dqkv, dk, dv)
    self_backward(1, qkv, lse, datt4, dqkv, dk, dv)
    next(fl_b)
    next(fl_a)
    v13[...] = jnp.zeros_like(v13)
    v13[0:16, :] = sums[...]
    gain, shift = vec[0:1, :], vec[3:4, :]

    def norm_rows(i):
        r = pl.ds(pl.multiple_of(i * 128, 128), 128)
        z, _ = normed(x_all[r, :].astype(F32))
        n1[r, :] = (z * gain + shift).astype(BF)
        d = mm_cols(dqkv[r, :], wq[:, 0:768])
        dn[r, :] = d.astype(BF)
        v13[0:1, :] += jnp.sum(d * z, axis=0, keepdims=True)
        v13[3:4, :] += jnp.sum(d, axis=0, keepdims=True)

    loop(8, norm_rows)
    dns = [copies.start(dn.at[pl.ds(pl.multiple_of(to["y"] * 256, 256), 256)], dn4.at[k], to) for k, to in enumerate(row)]
    for f in fl_c:
        next(f)

    def grad_q(z):
        cols = pl.ds(pl.multiple_of(z * 256, 256), 256)
        gq[z, :, :, :, :, 0:768] = mm_rows(n1[:, cols], dqkv[...]).reshape(4, 2, 4, 8, 768).astype(BF)
        gq[z, :, :, :, :, 768:1280] = mm_rows(e[:, cols], dckv4[0]).reshape(4, 2, 4, 8, 512).astype(BF)

    loop(4, grad_q)
    gq[:, :, :, :, :, 1280:1408] = v13[...].T.reshape(4, 4, 2, 4, 8, 128).astype(BF)
    gq[:, :, :, :, :, 1408:1536] = jnp.zeros((4, 4, 2, 4, 8, 128), BF)
    n_q = gq.shape[-1]
    pq = copies.start(gq.at[:, :, :, :, :, half(n_q, partner)], gql, partner)
    next(fl_b)
    next(fl_a)
    pq.wait()
    mine = gq.at[:, :, :, :, :, half(n_q, at)]
    add_into(mine, gql)
    q_cols = lambda k: gq.at[:, :, :, :, :, pl.ds(pl.multiple_of(c * 768 + k * 384, 128), 384)]
    fl_q = [scatter_flow(q_cols(0), lq0, at, ("x", "z"), every, copies), scatter_flow(q_cols(1), lq1, at, ("z", "x"), every, copies)]
    for f in fl_q + fl_q + fl_c + [fl_b, fl_a] + fl_q:
        next(f)
    for s in dns + caps + [cap_own]:
        s.wait()

    def token_rows(i):
        r = pl.ds(pl.multiple_of(i * 64, 64), 64)
        here = pl.ds(pl.multiple_of(y * 256 + i * 64, 64), 64)
        d = dn[here, :].astype(F32) + dn4[0, r, :].astype(F32) + dn4[1, r, :].astype(F32) + dn4[2, r, :].astype(F32)
        back, _, _ = norm_back(x_all[here, :].astype(F32), d, gain)
        tok[r, :] = dx1[r, :] + back

    loop(4, token_rows)
    cap[...] = sum(dcap4[k].astype(F32) for k in range(4))
    finish(fl_c + [fl_b, fl_a] + fl_q)

    last = []
    for g, f in ((ga, fa), (gb, fb), (gc, fc)):
        last.append(copies.start(g.at[at["z"], at["x"], partner["c"], y], f, partner))
    for o in ring:
        last.append(copies.start(mine.at[at["z"], at["x"], o["c"], o["y"]], fq.at[c, y], o))
    own_q = load(mine.at[at["z"], at["x"], c, y], fq.at[c, y])
    for g, o in ((ga, out_a), (gb, out_b), (gc, out_c)):
        o[c] = g[at["z"], at["x"], c, y]
    for s in last + [own_q]:
        s.wait()
    for f, o in ((fa, out_a), (fb, out_b), (fc, out_c)):
        o[partner["c"]] = f[...]
    out_q[...] = fq[...]


def reduced(u, dy, n3, dh, att, r1, n2, dcq, catt, r2, datt, dckv, sums, x_all, qkv, lse, wq, e, dx1, vec):
    n_c, n_q = 1536, 768
    V = pltpu.VMEM
    scratch = [
        V((512, 4096), BF), V((512, 512), BF), V((512, 1024), BF), V((512, 2048), BF), V((3, 512, 1024), BF), V((3, 512, 512), BF),
        V((4, 4, 2, 4, 32, 512), BF), V((4, 4, 2, 4, 8, 2048), BF), V((4, 4, 2, 4, 8, n_c), BF),
        V((4, 4, 2, 4, 8, 2 * n_q), BF), V((4, 4, 2, 4, 8, n_q), BF),
        V((1024, 256), BF), V((4, 128, 512), BF), V((128, 1024), BF), V((4, 128, 256), BF), V((1024, 768), BF), V((1024, 1024), BF),
        V((1024, 128), F32), V((1024, 128), F32), V((1024, 1024), BF), V((3, 256, 1024), BF), V((128, 1024), F32),
        V((1024, 1024), BF), V((1024, 768), BF), V((1024, 1280), BF), V((256, 1024), F32),
    ]
    scratch += [landing_shapes(32, 512, "xzy"), landing_shapes(8, 2048, "zxy")]
    scratch += [landing_shapes(8, 512, axes) for axes in ("zxy", "xzy", "yzx")] + [landing_shapes(8, 384, axes) for axes in ("xz", "zx")]
    scratch += [V((32, 512), BF), V((8, 2048), BF), V((8, n_c), BF), V((2, 4, 8, n_q), BF)]
    n = 160
    scratch += [pltpu.SemaphoreType.DMA((n,)), pltpu.SemaphoreType.DMA((n,)), pltpu.SemaphoreType.DMA((32,))]
    s = jax.ShapeDtypeStruct
    outs = [s((2, 32, 512), BF), s((2, 8, 2048), BF), s((2, 8, n_c), BF), s((2, 4, 8, n_q), BF), s((256, 1024), F32), s((128, 256), F32)]
    anywhere, vm = pl.BlockSpec(memory_space=pl.ANY), pl.BlockSpec(memory_space=pltpu.VMEM)
    return pl.pallas_call(
        reduce_kernel, out_shape=outs, in_specs=[anywhere] * 12 + [vm, anywhere, anywhere, vm, anywhere, vm, anywhere, vm], out_specs=[vm] * 6,
        scratch_shapes=scratch,
        compiler_params=pltpu.CompilerParams(collective_id=1, has_side_effects=True, vmem_limit_bytes=62 << 20),
        name="reduce_gradients",
    )(u, dy, n3, dh, att, r1, n2, dcq, catt, r2, datt, dckv, sums, x_all, qkv, lse, wq, e, dx1, vec)


def finish_kernel(a, b, c, q, tok_in, cap_in, tok, cap, d_qkv, d_self_out, d_cross_q, d_cross_kv, d_cross_out, d_in, d_out, d_gains, d_shifts, d_biases, d_in_bias):
    tok[...] = tok_in[...]
    cap[...] = cap_in[...]
    for k in range(2):
        d_out[:, k * 512:(k + 1) * 512] = a[k].astype(F32)
        d_in[:, k * 2048:(k + 1) * 2048] = b[k].astype(F32)
        for m, ref in enumerate((d_cross_out, d_cross_q, d_self_out)):
            ref[:, k * 512:(k + 1) * 512] = c[k, :, m * 512:(m + 1) * 512].astype(F32)
    for y in range(4):
        for m in range(3):
            d_qkv[:, m * 1024 + y * 256:m * 1024 + (y + 1) * 256] = q[0, y, :, m * 256:(m + 1) * 256].astype(F32)
        for m in range(2):
            d_cross_kv[:, m * 1024 + y * 256:m * 1024 + (y + 1) * 256] = q[1, y, :, m * 256:(m + 1) * 256].astype(F32)
    vectors = sum(q[1, y, :, 512:640].astype(F32) for y in range(4)).T
    for m, ref in enumerate((d_gains, d_shifts, d_biases)):
        ref[...] = vectors[3 * m:3 * m + 3, :]
    d_in_bias[...] = jnp.concatenate([vectors[9 + j:10 + j, :] for j in range(4)], axis=1)


def assembled(a, b, c, q, tok, cap):
    shapes = [(256, 1024), (128, 256), (8, 3072), (8, 1024), (8, 1024), (8, 2048), (8, 1024), (8, 4096), (32, 1024), (3, 8), (3, 8), (3, 8), (1, 32)]
    vm = pl.BlockSpec(memory_space=pltpu.VMEM)
    return pl.pallas_call(
        finish_kernel, out_shape=[jax.ShapeDtypeStruct(s, F32) for s in shapes], in_specs=[vm] * 6, out_specs=[vm] * 13, name="assemble",
    )(a, b, c, q, tok, cap)


def local(tokens, captions, cap_lengths, w_qkv, w_self_out, w_cross_q, w_cross_kv, w_cross_out, w_in, w_out,
          norm_gains, norm_shifts, out_biases, in_bias, out_grad):
    vectors = jnp.concatenate([norm_gains.T, norm_shifts.T, out_biases.T, in_bias.reshape(4, 8).T], axis=1)
    vectors = jnp.pad(vectors, ((0, 0), (0, 128 - 13)))
    dy = out_grad[0]
    (c_g, win_g, wout_g, dy_pair, x_g, wq, qkv, lse, att, ck, cv, e, x1, x2, n2, n3, catt, probs, cq, vec, wide) = gathered(
        cap_lengths, w_qkv, w_cross_kv, w_self_out, w_cross_q, w_cross_out, vectors, w_in, w_out, tokens[0], captions[0], dy)
    wc, full_in, full_out = c_g.reshape(1024, -1), win_g.reshape(1024, -1), wout_g.reshape(4096, 1024)
    layer_out, dx1, datt, dckv, u, dh, r1, dcq, r2, sums = middle(
        x2, n3, dy, vec, wide, x1, probs, cq, ck, cv, wc, full_in, full_out)
    out_a, out_b, out_c, out_q, tokens_grad, captions_grad = reduced(
        u, dy_pair, n3, dh, att, r1, n2, dcq, catt, r2, datt, dckv, sums, x_g.reshape(1024, 1024), qkv, lse, wq, e, dx1, vec)
    tokens_grad, captions_grad, *grads, d_in_bias = assembled(out_a, out_b, out_c, out_q, tokens_grad, captions_grad)
    return (layer_out[None], tokens_grad[None], captions_grad[None], *grads, d_in_bias.reshape(32))


def solution(mesh):
    rows, tokens, vectors = P(("dp", "seq"), None), P("dp", "seq", None), P(None, ("dp", "seq"))
    captions = P("dp", None, "seq")
    return jax.shard_map(
        local, mesh=mesh,
        in_specs=(tokens, captions, P("dp"), *[rows] * 7, *[vectors] * 3, P(("dp", "seq")), tokens),
        out_specs=(tokens, tokens, captions, *[rows] * 7, *[vectors] * 3, P(("dp", "seq"))),
        check_vma=False,
    )
```

time: 234 us -> 222 us (0.949)
  other arithmetic: 6.72 us -> 0.66 us
  local copies, waits for them, and re-layouts: 9.07 us -> 3.94 us
    pallas_call x1, Pallas kernels: 94.1 us -> 85.1 us  [reduced(): pl.pallas_call(reduce_kernel, out_shape=outs, in_specs=[anywhere] * 12 +...]
    pallas_call x2, Pallas kernels: 120 us -> 129 us  [the longest x1 95 us: gathered(): pl.pallas_call(gather_kernel, out_shape=outs, in_specs=[pl.BlockSpec(memo...]
    concatenate x4 -> x0, other arithmetic: 4.6 us -> none  [the longest x1 1.75 us: local(): jnp.concatenate([sums[:9], d_hidden, jnp.zeros((115, 1024), jnp.float32)]...]
    reshape x6 -> x0, local copies, waits for them, and re-layouts: 2.81 us -> none  [the longest x1 1.27 us: local(): d_in_bias.reshape(32)]
where the time goes in v2:
time: 222 us
  Pallas kernels  216 us (97%)
  local copies, waits for them, and re-layouts  3.94 us (2%)
    pallas_call x1, Pallas kernels, gathered(): pl.pallas_call(gather_kernel, out_shape=outs, in_specs=[pl.BlockSpec(memo...  95 us
    pallas_call x1, Pallas kernels, reduced(): pl.pallas_call(reduce_kernel, out_shape=outs, in_specs=[anywhere] * 12 +...  85.1 us
    pallas_call x1, Pallas kernels, middle(): pl.pallas_call(middle_kernel, out_shape=outs, in_specs=[vm, anywhere] + [...  33.5 us

profile of v2, /device:TPU:1, one launch (start us, length us, event | category | flops | bytes accessed | tf_op | source)
XLA Modules:
  0.0 222.1 jit_solution(17849043822878134600)
XLA Ops:
  1.3 0.7 reshape.46
  2.0 0.1 copy.32
  2.1 0.8 copy.29
  2.9 0.8 copy.30
  3.7 0.8 copy.31
  4.4 0.7 fusion.6.vectors
  5.1 95.0 %gather_and_attend.1 = (bf16[4,4,2,4,8,3072]{5,4,3,2,1,0:T(8,128)(2,1)}, bf16[4,4,2,4,8,4096]{5,4,3,2,1,0:T(8,128)(2,1)}, bf16[4,4,2,4,32,1024]{5,4,3,2,1,0:T(8,...) custom-call(s32[1]{0:T(128)S(6)} %copy.34.length, ...), custom_call_target="tpu_custom_call" | custom-call | tf_op jit(solution)/shard_map/gather_and_attend/pallas_call | solution.py:387
  100.1 33.5 %middle.1 = (bf16[256,1024]{1,0:T(8,128)(2,1)}, f32[256,1024]{1,0:T(8,128)}, bf16[256,1024]{1,0:T(8,128)(2,1)}, bf16[128,2048]{1,0:T(8,128)(2,1)}, bf16[512,4096...) custom-call(f32[256,1024]{1,0:T(8,128)} %get-tuple-element.64.x2_in,, ...), custom_call_target="tpu_custom_call" | custom-call | tf_op jit(solution)/shard_map/middle/pallas_call | solution.py:550
  133.6 0.0 copy-start
  133.6 85.1 %reduce_gradients.1 = (bf16[2,32,512]{2,1,0:T(8,128)(2,1)}, bf16[2,8,2048]{2,1,0:T(8,128)(2,1)}, bf16[2,8,1536]{2,1,0:T(8,128)(2,1)}, bf16[2,4,8,768]{3,2,1,0:T(...) custom-call(bf16[512,4096]{1,0:T(8,128)(2,1)} %get-tuple-element.77.u, bf16[512,512]{1,0:T(8,128)(2,1)} %get-tuple-element.78.dy, ...), custom_call_target="tpu_custom_call" | custom-call | tf_op jit(solution)/shard_map/reduce_gradients/pallas_call | solution.py:807
  218.7 2.6 %assemble.1 = (f32[256,1024]{1,0:T(8,128)}, f32[128,256]{1,0:T(8,128)}, f32[8,3072]{1,0:T(8,128)}, f32[8,1024]{1,0:T(8,128)}, f32[8,1024]{1,0:T(8,128)}, /*index...) custom-call(bf16[2,32,512]{2,1,0:T(8,128)(2,1)} %get-tuple-element.9, ...), custom_call_target="tpu_custom_call" | custom-call | tf_op jit(solution)/shard_map/assemble/pallas_call | solution.py:837
  221.3 0.0 copy-done
  221.3 0.8 copy.35
Async XLA Ops:
  133.6 87.7 %copy-start = (bf16[256,1024]{1,0:T(8,128)(2,1)S(1)}, bf16[256,1024]{1,0:T(8,128)(2,1)}, u32[]{:S(2)}) copy-start(bf16[256,1024]{1,0:T(8,128)(2,1)} %get-tuple-element.76) | copy-start | bytes 1572868
